TPU v7x, 32 devices: a whole 2x2x4 slice. The times are simulated.
32 devices in a mesh: gx: 4 (over z), yz: 8 (over y, x, core).
Axes of the slice: x: 2, y: 2, z: 4, core: 2. Of those that a mesh axis runs over, the one named last changes fastest.
Arguments:
- fields: float32 [5, 256, 96, 512], P(None, 'yz', None, 'gx'), may hold values from -6 to 6
- inflow: float32 [5, 256, 96], P(None, 'yz'), may hold values from -6 to 6
- rates_fwd: float32 [256, 96, 512], P('yz', None, 'gx'), may hold values from 0.45 to 1
- rates_bwd: float32 [256, 96, 512], P('yz', None, 'gx'), may hold values from 0.45 to 1
- flux_wall: float32 [5, 5], replicated, may hold values from -2.5 to 2.5
- flux_span: float32 [5, 5], replicated, may hold values from -2.5 to 2.5
- viscosity: float32 [5], replicated, may hold values from 0.05 to 0.5
Outputs:
- advanced: float32 [5, 256, 96, 512], P(None, 'yz', None, 'gx')
All inputs are finite; a program needn't handle non-finite values.
Results may differ from a plain program's by a relative error of at most 0.00018.
Values sent between devices are 32-bit elements; how exact they have to be, the bound alone decides.
No kernel may reach another device: no remote copies, remote signals or barrier semaphores. Data moves between devices by JAX's collectives and lax.ppermute only.
A program may use at most 256 MiB of HBM per device.

v0:
```python
import math

import jax
import jax.numpy as jnp
from jax import lax
from jax.sharding import PartitionSpec as P

ALPHA_D = 0.25
ALPHA_F = 0.499
TIME_STEP = 0.5


def prefix(value, axis, join, neutral, backward):
    count, mine = (lax.axis_size(axis), lax.axis_index(axis))
    pieces = jax.tree.map(lambda part: lax.all_gather(part, axis), value)
    if backward:
        pieces = jax.tree.map(lambda part: part[::-1], pieces)
        mine = count - 1 - mine
    running = jax.tree.map(
        lambda part, zero: jnp.full_like(part, 0) + jnp.asarray(zero, part.dtype), value, neutral
    )

    def lap(position, running):
        longer = join(running, jax.tree.map(lambda part: part[position], pieces))
        return jax.tree.map(lambda new, old: jnp.where(position < mine, new, old), longer, running)

    return lax.fori_loop(0, count - 1, lap, running)


def root_of(coupling):
    return (-1.0 + math.sqrt(1.0 - 4.0 * coupling * coupling)) / (2.0 * coupling)


def signed_power(exponent, ratio):
    magnitude = jnp.exp(exponent.astype(jnp.float32) * math.log(abs(ratio)))
    parity = jnp.where(exponent % 2 == 0, 1.0, -1.0).astype(jnp.float32)
    return magnitude * parity


def inverse_of(points, coupling, periodic):
    ratio = root_of(coupling)
    row_idx = lax.broadcasted_iota(jnp.int32, (points, points), 0)
    col_idx = lax.broadcasted_iota(jnp.int32, (points, points), 1)
    if periodic:
        offset = (col_idx - row_idx) % points
        factor = 1.0 / ((1.0 + 2.0 * coupling * ratio) * (1.0 - ratio**points))
        return factor * (signed_power(offset, ratio) + signed_power(points - offset, ratio))
    near_idx = jnp.minimum(row_idx, col_idx)
    far_idx = jnp.maximum(row_idx, col_idx)
    factor = 1.0 / ((1.0 + 2.0 * coupling * ratio) * (1.0 - ratio ** (2 * points + 2)))
    numerator = signed_power(far_idx - near_idx, ratio) * (
        1.0 - signed_power(2 * near_idx + 2, ratio)
    )
    numerator = numerator * (1.0 - signed_power(2 * points - 2 * far_idx, ratio))
    return factor * numerator


def band_of(points, below, centre, above, periodic):
    row_idx = lax.broadcasted_iota(jnp.int32, (points, points), 0)
    col_idx = lax.broadcasted_iota(jnp.int32, (points, points), 1)
    offset = col_idx - row_idx
    if periodic:
        offset = (offset + 1) % points - 1
    values = jnp.where(
        offset == 0, centre, jnp.where(offset == 1, above, jnp.where(offset == -1, below, 0.0))
    )
    return values.astype(jnp.float32)


def operators(points, periodic):
    highest = lax.Precision.HIGHEST
    deriv_op = jnp.dot(
        inverse_of(points, ALPHA_D, periodic),
        band_of(points, -0.75, 0.0, 0.75, periodic),
        precision=highest,
    )
    half_side = 0.5 * (0.5 + ALPHA_F)
    filter_op = jnp.dot(
        inverse_of(points, ALPHA_F, periodic),
        band_of(points, half_side, 0.5 + ALPHA_F, half_side, periodic),
        precision=highest,
    )
    deriv_filter = jnp.dot(deriv_op, filter_op, precision=highest)
    second_filter = jnp.dot(deriv_op, deriv_filter, precision=highest)
    return jnp.stack([filter_op, deriv_filter, second_filter])


def mix_fields(matrix, values):
    return jnp.einsum("fg,gyzx->fyzx", matrix, values, precision=lax.Precision.HIGHEST)


def compose(earlier, later):
    gain_early, sum_early = earlier
    gain_late, sum_late = later
    return (gain_early * gain_late, gain_late * sum_early + sum_late)


def shards(fields, inflow, rates_fwd, rates_bwd, flux_wall, flux_span, viscosity):
    highest = lax.Precision.HIGHEST
    wall_devs = lax.axis_size("yz")
    span_cells = fields.shape[2]
    height = fields.shape[1] * wall_devs
    span_ops = operators(span_cells, True)
    wall_ops = operators(height, False)
    visc_col = viscosity[:, None, None, None]
    along_z = jnp.einsum("kab,fybx->kfyax", span_ops, fields, precision=highest)
    spanwise = -mix_fields(flux_span, along_z[1]) + visc_col * along_z[2]
    smooth = lax.all_to_all(along_z[0], "yz", split_axis=2, concat_axis=1, tiled=True)
    span_part = lax.all_to_all(spanwise, "yz", split_axis=2, concat_axis=1, tiled=True)
    stacked = jnp.einsum("kab,fbzx->kfazx", wall_ops, smooth, precision=highest)
    span_filtered = jnp.einsum("ab,fbzx->fazx", wall_ops[0], span_part, precision=highest)
    combined = stacked[0] + TIME_STEP * (
        span_filtered - mix_fields(flux_wall, stacked[1]) + visc_col * stacked[2]
    )
    right_side = lax.all_to_all(combined, "yz", split_axis=1, concat_axis=2, tiled=True)
    n_fields, wall_rows, span_rows, x_cells = right_side.shape
    line_count = wall_rows * span_rows
    sections = lax.axis_size("gx")
    section = lax.axis_index("gx")
    flat_rhs = jnp.transpose(right_side, (3, 0, 1, 2)).reshape(x_cells, n_fields, line_count)
    flat_fwd = jnp.transpose(rates_fwd, (2, 0, 1)).reshape(x_cells, 1, line_count)
    flat_bwd = jnp.transpose(rates_bwd, (2, 0, 1)).reshape(x_cells, 1, line_count)
    inflow_flat = inflow.reshape(n_fields, line_count)
    fwd_prod, fwd_sum = lax.associative_scan(
        compose, (flat_fwd, (1.0 - flat_fwd) * flat_rhs), axis=0
    )
    x_index = lax.broadcasted_iota(jnp.int32, flat_bwd.shape, 0)
    outlet = jnp.logical_and(x_index == x_cells - 1, section == sections - 1)
    bwd_rate = jnp.where(outlet, 0.0, flat_bwd)
    unit_map = (
        jnp.ones((1, line_count), jnp.float32),
        jnp.zeros((n_fields, line_count), jnp.float32),
    )
    below_map = prefix((fwd_prod[-1], fwd_sum[-1]), "gx", compose, unit_map, False)
    entering = below_map[0] * inflow_flat + below_map[1]
    forward = fwd_prod * entering[None] + fwd_sum
    bwd_prod, bwd_sum = lax.associative_scan(
        compose, (bwd_rate, (1.0 - bwd_rate) * forward), reverse=True, axis=0
    )
    above_map = prefix((bwd_prod[0], bwd_sum[0]), "gx", compose, unit_map, True)
    advanced_flat = bwd_prod * above_map[1][None] + bwd_sum
    advanced = jnp.transpose(
        advanced_flat.reshape(x_cells, n_fields, wall_rows, span_rows), (1, 2, 3, 0)
    )
    return advanced


def solution(mesh):
    placed = (
        P(None, "yz", None, "gx"),
        P(None, "yz", None),
        P("yz", None, "gx"),
        P("yz", None, "gx"),
        P(),
        P(),
        P(),
    )
    return jax.shard_map(
        shards, mesh=mesh, in_specs=placed, out_specs=P(None, "yz", None, "gx"), check_vma=False
    )
```

profile of v0, /device:TPU:0, one launch (start us, length us, event | category | flops | bytes accessed | tf_op | source)
XLA Modules:
  0.0 1754.2 jit_solution(14826708341133697389)
XLA Ops:
  1.0 23.6 %convolution_bitcast_fusion.1 = f32[3,5,32,96,128]{4,3,2,1,0:T(8,128)} fusion(f32[5,32,96,128]{3,2,1,0:T(8,128)} %param.11, f32[1,96,96]{2,1,0:T(8,128)S(1)} %convolution_bitcast_fusion.3, f32[1,96,96]{2,1,0:T(8,128)S(1)} %bitcast.223, f32[1,96,96]{2,1,0:T(8,128)S(1)} %bitcast.225), kind=kOutput, calls=%fused_computation.11 | convolution fusion | flops 6794827776 | bytes 31567872 | tf_op jit(solution)/shard_map/kab,fybx->kfyax/dot_general | solution.py:106
  37.4 21.8 %fusion.2 = f32[32,96,128,5]{2,3,1,0:T(8,128)} fusion(f32[5,32,96,128]{3,2,1,0:T(8,128)} %get-tuple-element.297, f32[5,5]{1,0:T(8,128)S(1)} %copy-done), kind=kOutput, calls=%fused_computation.8 | convolution fusion | flops 117964800 | bytes 15728740 | tf_op jit(solution)/shard_map/fg,gyzx->fyzx/dot_general | solution.py:89
  88.2 30.3 %slice.523 = f32[63,1,3072]{0,2,1:T(8,128)} slice(f32[128,1,3072]{0,2,1:T(8,128)S(1)} %bitcast.178), slice={[2:128:2], [0:1:1], [0:3072:1]} | slice | bytes 1548288 | tf_op jit(solution)/shard_map/slice | solution.py:124
  118.5 30.6 %slice.494 = f32[64,1,3072]{0,2,1:T(8,128)} slice(f32[128,1,3072]{0,2,1:T(8,128)S(1)} %bitcast.179), slice={[1:128:2], [0:1:1], [0:3072:1]} | slice | bytes 1572864 | tf_op jit(solution)/shard_map/slice | solution.py:124
  150.7 28.3 %slice.458 = f32[64,1,3072]{0,2,1:T(8,128)} slice(f32[128,1,3072]{0,2,1:T(8,128)S(1)} %bitcast_select_fusion), slice={[0:127:2], [0:1:1], [0:3072:1]} | slice | bytes 1572864 | tf_op jit(solution)/shard_map/slice | solution.py:137
  179.0 30.6 %slice.456 = f32[64,1,3072]{0,2,1:T(8,128)} slice(f32[128,1,3072]{0,2,1:T(8,128)S(1)} %bitcast_select_fusion), slice={[1:128:2], [0:1:1], [0:3072:1]} | slice | bytes 1572864 | tf_op jit(solution)/shard_map/slice | solution.py:137
  233.8 15.4 slice.462
  249.3 15.1 slice.461
  334.1 28.4 %slice.493 = f32[64,1,3072]{0,2,1:T(8,128)} slice(f32[128,1,3072]{0,2,1:T(8,128)S(1)} %bitcast.180), slice={[0:127:2], [0:1:1], [0:3072:1]} | slice | bytes 1572864 | tf_op jit(solution)/shard_map/slice | solution.py:124
  364.5 15.1 slice.521
  379.6 15.4 slice.497
  395.0 15.1 slice.496
  605.0 15.1 pad.196
  620.1 18.4 %pad.197 = f32[64,1,3072]{0,2,1:T(8,128)} pad(f32[32,1,3072]{0,2,1:T(8,128)} %add.440, f32[]{:T(128)} %constant.150.clone.1), padding=1_0_1x0_0_0x0_0_0 | pad | bytes 1179652 | tf_op jit(solution)/shard_map/pad | solution.py:124
  641.3 31.5 %pad.199 = f32[128,1,3072]{0,2,1:T(8,128)} pad(f32[64,1,3072]{0,2,1:T(8,128)} %add.441, f32[]{:T(128)} %constant.150.clone.1), padding=1_0_1x0_0_0x0_0_0 | pad | bytes 2359300 | tf_op jit(solution)/shard_map/pad | solution.py:124
  677.2 31.3 %pad.198 = f32[128,1,3072]{0,2,1:T(8,128)} pad(f32[64,1,3072]{0,2,1:T(8,128)} %pad_maximum_fusion.15, f32[]{:T(128)} %constant.150.clone.1), padding=0_1_1x0_0_0x0_0_0 | pad | bytes 2359300 | tf_op jit(solution)/shard_map/pad | solution.py:124
  755.2 42.0 %convolution_bitcast_fusion = f32[3,5,256,12,128]{2,4,0,3,1:T(8,128)S(1)} fusion(f32[5,256,12,128,1]{3,1,4,2,0:T(8,128)} %bitcast.193, f32[1,256,256]{2,1,0:T(8,128)} %convolution_bitcast_fusion.2, f32[1,256,256]{2,1,0:T(8,128)} %bitcast.220, f32[1,256,256]{2,1,0:T(8,128)S(1)} %bitcast.219), kind=kOutput, calls=%fused_computation.10 | convolution fusion | flops 18119786496 | bytes 32243712 | tf_op jit(solution)/shard_map/kab,fbzx->kfazx/dot_general | solution.py:110
  820.3 16.4 fusion.200
  847.4 22.1 %fusion.7 = f32[5,256,12,128]{1,3,2,0:T(8,128)} fusion(f32[3,5,256,12,128]{2,4,0,3,1:T(8,128)} %copy-done.2, f32[256,12,128,5]{0,2,1,3:T(8,128)} %copy.261, f32[5]{0:T(128)S(1)} %copy-done.110, f32[5,256,12,128]{3,1,2,0:T(8,128)} %bitcast.192, f32[256,256]{1,0:T(8,128)S(1)} %fusion.33), kind=kOutput, calls=%fused_computation.16 | convolution fusion | flops 6049628160 | bytes 39583764 | tf_op jit(solution)/shard_map/ab,fbzx->fazx/dot_general | solution.py:111
  888.4 28.2 %slice.488 = f32[63,1,3072]{0,2,1:T(8,128)} slice(f32[128,1,3072]{0,2,1:T(8,128)S(1)} %copy-done.5), slice={[1:126:2], [0:1:1], [0:3072:1]} | slice | bytes 1548288 | tf_op jit(solution)/shard_map/slice | solution.py:137
  918.3 15.0 slice.486
  1108.5 15.3 pad.182
  1123.8 15.7 pad.183
  1143.4 26.0 %pad.184 = f32[128,1,3072]{0,2,1:T(8,128)S(1)} pad(f32[64,1,3072]{0,2,1:T(8,128)S(1)} %pad_maximum_fusion.9, f32[]{:T(128)} %constant.150.clone.1), padding=0_1_1x0_0_0x0_0_0 | pad | bytes 2359300 | tf_op jit(solution)/shard_map/pad | solution.py:137
  1169.4 28.8 %pad.185 = f32[128,1,3072]{0,2,1:T(8,128)S(1)} pad(f32[64,1,3072]{0,2,1:T(8,128)} %add.434, f32[]{:T(128)} %constant.150.clone.1), padding=1_0_1x0_0_0x0_0_0 | pad | bytes 2359300 | tf_op jit(solution)/shard_map/pad | solution.py:137
  1207.3 14.4 all_gather.12
  1222.3 14.3 all_gather.13
  1427.9 15.9 all_gather.14
  1499.9 14.1 slice.566
  1567.1 14.2 slice.598
  1659.4 60.5 %rev.17 = f32[128,5,3072]{2,0,1:T(8,128)} reverse(f32[128,5,3072]{2,0,1:T(8,128)} %add.498), dimensions={0} | reverse | bytes 15728640 | tf_op jit(solution)/shard_map/rev | solution.py:137
  1719.9 14.4 all_gather.15
  (529 shorter events, 1036.8 us)
Async XLA Ops:
  0.0 37.4 %copy-start = (f32[5,5]{1,0:T(8,128)S(1)}, f32[5,5]{1,0:T(8,128)}, u32[]{:S(2)}) copy-start(f32[5,5]{1,0:T(8,128)} %param.16) | copy-start | bytes 304
  37.4 21.8 %copy-start.109 = (f32[5]{0:T(128)S(1)}, f32[5]{0:T(128)}, u32[]{:S(2)}) copy-start(f32[5]{0:T(128)} %param.17) | copy-start | bytes 64
  82.5 513.2 %all-to-all-start.1 = ((f32[5,32,96,128]{3,1,0,2:T(8,128)}), f32[5,32,96,128]{3,1,0,2:T(8,128)}, u32[]{:S(2)}, u32[]{:S(2)}) async-start(f32[5,32,96,128]{3,1,0,2:T(8,128)} %copy.256), calls=%async_computation.1 | async-start | bytes 15728640 | tf_op jit(solution)/shard_map/all_to_all | solution.py:109
  150.7 28.3 %copy-start.4 = (f32[128,1,3072]{0,2,1:T(8,128)}, f32[128,1,3072]{0,2,1:T(8,128)S(1)}, u32[]{:S(2)}) copy-start(f32[128,1,3072]{0,2,1:T(8,128)S(1)} %bitcast_select_fusion) | copy-start | bytes 4718596
  209.6 13.5 copy-start.67
  233.8 15.5 copy-start.8
  302.5 12.4 copy-start.14
  364.5 30.5 %copy-start.15 = (f32[64,1,3072]{0,2,1:T(8,128)}, f32[64,1,3072]{0,2,1:T(8,128)S(1)}, u32[]{:S(2)}) copy-start(f32[64,1,3072]{0,2,1:T(8,128)S(1)} %mul.595) | copy-start | bytes 2359300
  412.1 17.8 %copy-start.17 = (f32[32,1,3072]{0,2,1:T(8,128)}, f32[32,1,3072]{0,2,1:T(8,128)S(1)}, u32[]{:S(2)}) copy-start(f32[32,1,3072]{0,2,1:T(8,128)S(1)} %mul.596) | copy-start | bytes 1179652
  440.8 14.2 copy-start.19
  463.9 12.4 copy-start.21
  571.3 23.0 %copy-start.50 = (f32[32,1,3072]{0,2,1:T(8,128)}, f32[32,1,3072]{0,2,1:T(8,128)S(1)}, u32[]{:S(2)}) copy-start(f32[32,1,3072]{0,2,1:T(8,128)S(1)} %pad.194) | copy-start | bytes 1179652
  583.2 11.1 copy-start.51
  595.7 151.7 %all-to-all-start = ((f32[5,32,96,128]{3,1,0,2:T(8,128)}), f32[5,32,96,128]{3,1,0,2:T(8,128)}, u32[]{:S(2)}, u32[]{:S(2)}) async-start(f32[5,32,96,128]{3,1,0,2:T(8,128)} %copy.249), calls=%async_computation | async-start | bytes 15728640 | tf_op jit(solution)/shard_map/all_to_all | solution.py:108
  620.1 18.4 %copy-start.53 = (f32[64,1,3072]{0,2,1:T(8,128)}, f32[64,1,3072]{0,2,1:T(8,128)S(1)}, u32[]{:S(2)}) copy-start(f32[64,1,3072]{0,2,1:T(8,128)S(1)} %pad.196) | copy-start | bytes 2359300
  808.9 11.4 copy-start.106
  880.9 357.3 %all-to-all-start.2 = ((f32[5,256,12,128]{3,2,0,1:T(8,128)}), f32[5,256,12,128]{3,2,0,1:T(8,128)}, u32[]{:S(2)}, u32[]{:S(2)}) async-start(f32[5,256,12,128]{3,2,0,1:T(8,128)} %copy.262), calls=%async_computation.2 | async-start | bytes 20971520 | tf_op jit(solution)/shard_map/all_to_all | solution.py:115
  918.3 15.0 copy-start.11
  1205.6 30.9 %copy-start.108 = (pred[128]{0:T(512)(128)(4,1)S(1)}, pred[128]{0:T(512)(128)(4,1)}, u32[]{:S(2)}) copy-start(pred[128]{0:T(512)(128)(4,1)} %copy-done.107) | copy-start | bytes 388
  1296.7 12.8 copy-start.79
  1382.4 12.8 copy-start.77
  1413.7 30.1 %copy-start.73 = (f32[5,3072]{1,0:T(8,128)S(1)}, f32[5,3072]{1,0:T(8,128)}, u32[]{:S(2)}) copy-start(f32[5,3072]{1,0:T(8,128)} %custom-call.1) | copy-start | bytes 184324
  1413.7 35.5 %copy-start.65 = (f32[128,3072]{1,0:T(8,128)S(1)}, f32[128,3072]{1,0:T(8,128)}, u32[]{:S(2)}) copy-start(f32[128,3072]{1,0:T(8,128)} %copy.246) | copy-start | bytes 4718596
  1426.5 22.6 %copy-start.90 = (f32[5,3072]{1,0:T(8,128)S(1)}, f32[5,3072]{1,0:T(8,128)}, u32[]{:S(2)}) copy-start(f32[5,3072]{1,0:T(8,128)} %reshape.87) | copy-start | bytes 184324
  1514.0 14.0 copy-start.78
  1565.3 15.9 copy-start.75
  1567.1 14.2 copy-start.99
  1567.1 14.3 copy-start.104
  1567.1 14.5 copy-start.102
  1602.8 12.9 copy-start.76
  1659.4 75.0 %copy-start.72 = (f32[5,3072]{1,0:T(8,128)S(1)}, f32[5,3072]{1,0:T(8,128)}, u32[]{:S(2)}) copy-start(f32[5,3072]{1,0:T(8,128)} %custom-call.2) | copy-start | bytes 184324
  1719.9 16.9 copy-start.64
  (84 other events, 269.8 us)
where the time goes:
time: 1780 us; the launch traced here: 1750 us
  local copies, waits for them, and re-layouts  1330 us (75%)
  other arithmetic  214 us (12%)
  matrix products  130 us (7%)
  blocking collectives  58.9 us (3%)
    slice x47, local copies, waits for them, and re-layouts, shards(): lax.associative_scan(compose, (bwd_rate, (1.0 - bwd_rate) * forward), rev...  360 us
    slice x40, local copies, waits for them, and re-layouts, shards(): lax.associative_scan(compose, (flat_fwd, (1.0 - flat_fwd) * flat_rhs), ax...  285 us
    pad x24, local copies, waits for them, and re-layouts, shards(): lax.associative_scan(compose, (flat_fwd, (1.0 - flat_fwd) * flat_rhs), ax...  203 us
    pad x24, local copies, waits for them, and re-layouts, shards(): lax.associative_scan(compose, (bwd_rate, (1.0 - bwd_rate) * forward), rev...  191 us
    rev x2, local copies, waits for them, and re-layouts, shards(): lax.associative_scan(compose, (bwd_rate, (1.0 - bwd_rate) * forward), rev...  62.6 us
    all_gather x4, blocking collectives, prefix(): pieces = jax.tree.map(lambda part: lax.all_gather(part, axis), value)  58.9 us
    mul x22, local copies, waits for them, and re-layouts, compose(): return (gain_early * gain_late, gain_late * sum_early + sum_late)  56.7 us
    dot_general x1, matrix products, shards(): stacked = jnp.einsum('kab,fbzx->kfazx', wall_ops, smooth, precision=highest)  42 us
  transfers between devices with their start and end apart: 3, of which 0 were waited for; matrix products, arithmetic and copies ran while one was open for 55% of the time, Pallas kernels for 0%

commit v1 on v0

v1 whole, which is shorter than its diff:
```python
import functools

import jax
import jax.numpy as jnp
import numpy as np
from jax import lax
from jax.experimental import pallas as pl
from jax.experimental.pallas import tpu as pltpu
from jax.sharding import PartitionSpec as P

F32, BF16 = jnp.float32, jnp.bfloat16
STEP = 0.5
LIMITS = {"mats": 56, "taps": 56, "chip": 8, "span": 12, "rates": 12, "states": 10, "sweep": 56, "close": 56}


def tridiagonal(points, below, centre, above, periodic):
    band = centre * np.eye(points) + below * np.eye(points, k=-1) + above * np.eye(points, k=1)
    if periodic:
        band[0, -1] += below
        band[-1, 0] += above
    return band


def operators(points, periodic):
    deriv = np.linalg.solve(
        tridiagonal(points, 0.25, 1.0, 0.25, periodic),
        tridiagonal(points, -0.75, 0.0, 0.75, periodic),
    )
    smooth = np.linalg.solve(
        tridiagonal(points, 0.499, 1.0, 0.499, periodic),
        tridiagonal(points, 0.4995, 0.999, 0.4995, periodic),
    )
    return smooth, deriv @ smooth, deriv @ deriv @ smooth


def wall_tables(points, devs):
    ops = operators(points, False)
    rows = points // devs

    def frame(first):
        vecs = np.stack(first)
        basis = []
        for vec in vecs:
            for _ in range(3):
                for other in basis:
                    vec = vec - other * (other @ vec)
            basis.append(vec / np.linalg.norm(vec))
        return np.stack(basis)

    above, below = {}, {}
    for edge in range(rows, points, rows):
        above[edge] = np.zeros((3, points))
        above[edge][:, edge:] = frame([op[edge - 1, edge:] for op in ops])
        below[edge] = np.zeros((3, points))
        below[edge][:, :edge] = frame([op[edge, :edge] for op in ops])
    nothing = np.zeros((3, points))
    above_at = lambda edge: above.get(edge, nothing)
    below_at = lambda edge: below.get(edge, nothing)

    def carry_above(target, source):
        return above_at(target) @ above_at(source).T

    def carry_below(target, source):
        return below_at(target) @ below_at(source).T

    chips = devs // 2
    taps = np.zeros((devs, 6, rows))
    local = np.zeros((devs, 3, rows, rows))
    reach = np.zeros((devs, 3, rows, 6))
    chip_mix = np.zeros((devs, 2, 3, 6))
    from_chip = np.zeros((devs, 2, max(chips - 1, 1), 3, 3))
    to_core = np.zeros((devs, 4, 3, 3))
    eye = np.eye(3)
    for dev in range(devs):
        low, high = dev * rows, (dev + 1) * rows
        own = slice(low, high)
        taps[dev, :3] = above_at(low)[:, own]
        taps[dev, 3:] = below_at(high)[:, own]
        for at, op in enumerate(ops):
            local[dev, at] = op[own, own]
            reach[dev, at, :, :3] = op[own] @ above_at(high).T
            reach[dev, at, :, 3:] = op[own] @ below_at(low).T
        chip, core = divmod(dev, 2)
        start, middle, end = 2 * chip * rows, (2 * chip + 1) * rows, (2 * chip + 2) * rows
        up = [eye, carry_above(start, middle)]
        down = [carry_below(end, middle), eye]
        chip_mix[dev, 0] = np.concatenate([up[core], up[1 - core]], 1)
        chip_mix[dev, 1] = np.concatenate([down[core], down[1 - core]], 1)
        for at in range(1, chips):
            other = chip ^ at
            if other > chip:
                from_chip[dev, 0, at - 1] = carry_above(end, 2 * other * rows)
            else:
                from_chip[dev, 1, at - 1] = carry_below(start, (2 * other + 2) * rows)
        above_core = [carry_above(middle, end), eye]
        below_core = [eye, carry_below(middle, start)]
        to_core[dev, 0], to_core[dev, 1] = above_core[core], above_core[1 - core]
        to_core[dev, 2], to_core[dev, 3] = below_core[core], below_core[1 - core]
    return taps, local, reach, chip_mix, from_chip, to_core


def wall_layout(local, reach, fields):
    devs, _, rows, _ = local.shape
    states = reach.transpose(0, 1, 3, 2)
    us = -(-6 * fields // 32) * 32
    ws = -(-(2 * fields * rows + us + 2 * fields) // 128) * 128 - 2 * fields * rows - us
    width = 2 * fields * rows + us + ws
    owner = np.full(width, -1)
    parts = np.zeros((devs, 3, rows, width))
    for field in range(fields):
        at = slice(field * rows, (field + 1) * rows)
        owner[at] = field
        parts[:, 1:, :, at] = local[:, 1:]
        at = slice(fields * rows + us + field * rows, fields * rows + us + (field + 1) * rows)
        owner[at] = field
        parts[:, 0, :, at] = local[:, 0]
        for k in range(6):
            at = fields * rows + k * fields + field
            owner[at] = field
            parts[:, 1:, :, at] = states[:, 1:, k]
        for place, k in enumerate((0, 3)):
            at = 2 * fields * rows + us + place * fields + field
            owner[at] = field
            parts[:, 0, :, at] = states[:, 0, k]
    pick = (owner[None] == np.arange(fields)[:, None]).astype(np.float64)
    tall = np.concatenate([parts] * fields, axis=2)
    same = np.repeat(pick, rows, axis=0)
    return tall[:, 1:], tall[:, 0] * same, pick, us, ws


def split(value):
    high = np.asarray(value, np.float32).astype(BF16)
    low = (np.asarray(value, np.float32) - high.astype(np.float32)).astype(BF16)
    return np.concatenate([high, high, low], axis=-1)


def parted(value):
    high = value.astype(BF16)
    return high, (value - high.astype(F32)).astype(BF16)


def dot(a, b):
    return jnp.dot(a, b, preferred_element_type=F32)


def stacked(value):
    high, low = parted(value)
    return jnp.concatenate([high, low, high], axis=0)


def padded(value, to):
    if value.shape[0] == to:
        return value
    return jnp.concatenate([value, jnp.zeros((to - value.shape[0], value.shape[1]), F32)], axis=0)


def running(value, twice):
    high, low = parted(value)
    return dot(jnp.concatenate([high, low], axis=1), twice)


def mats_kernel(fields, flux_wall_ref, flux_span_ref, visc_ref, wall_rows_ref, wall_cols_ref,
                wall_ref, wall_plain_ref, span_rows_ref, span_cols_ref, span_ref, span_plain_ref,
                wall_out, span_out):
    exact = functools.partial(jnp.dot, precision=lax.Precision.HIGHEST, preferred_element_type=F32)
    size = visc_ref.shape[1]
    here = lax.broadcasted_iota(jnp.int32, (size, size), 0) == lax.broadcasted_iota(
        jnp.int32, (size, size), 1)
    visc = jnp.where(here, STEP * visc_ref[...], 0.0)
    for flux_ref, rows_ref, cols_ref, ops, plain, out in (
        (flux_wall_ref, wall_rows_ref, wall_cols_ref, wall_ref[0], wall_plain_ref[0], wall_out),
        (flux_span_ref, span_rows_ref, span_cols_ref, span_ref[...], span_plain_ref[...], span_out),
    ):
        rows, cols = rows_ref[...], cols_ref[...]
        first = exact(exact(rows, -STEP * flux_ref[...]), cols)
        second = exact(exact(rows, visc), cols)
        high, low = parted(first * ops[0] + second * ops[1] + plain)
        width = cols.shape[1]
        out[:, :width] = high
        out[:, width : 2 * width] = high
        out[:, 2 * width :] = low


def mats_kernel_at(fields, dev_ref, *refs):
    mats_kernel(fields, *refs)


def taps_kernel(taps_ref, x_ref, keep_ref, send_ref):
    rows = x_ref.shape[1]
    me = lax.axis_index("yz")
    base = me * (6 * rows)
    half = x_ref.shape[2] // 2
    step = half if half <= 48 else 8
    core = me % 2
    for out_ref, offset in ((keep_ref, core * half), (send_ref, (1 - core) * half)):

        def piece(at, _):
            source = pl.multiple_of(offset + at * step, 8)
            sums = [None] * 6
            for row in range(rows):
                value = x_ref[0, row, pl.ds(source, step), :]
                for tap in range(6):
                    term = taps_ref[base + (tap * rows + row)] * value
                    sums[tap] = term if row == 0 else sums[tap] + term
            for tap in range(6):
                out_ref[tap, 0, pl.ds(pl.multiple_of(at * step, 8), step), :] = sums[tap]
            return 0

        lax.fori_loop(0, half // step, piece, 0)


def chip_kernel(chips, mix_ref, own_ref, other_ref, *out_refs):
    me = lax.axis_index("yz")
    chip, base = me // 2, me * 36
    lines = own_ref.shape[1]

    def piece(at, _):
        span = pl.ds(pl.multiple_of(at * 24, 8), 24)
        sums = []
        for side in range(2):
            terms = [own_ref[3 * side + k, span, :] for k in range(3)]
            terms += [other_ref[3 * side + k, span, :] for k in range(3)]
            sums.append(
                [sum(mix_ref[base + (18 * side + 6 * row + k)] * terms[k] for k in range(6)) for row in range(3)]
            )
        for at_chip in range(1, chips):
            lower = chip < (chip ^ at_chip)
            for row in range(3):
                out_refs[at_chip - 1][row, span, :] = jnp.where(lower, sums[1][row], sums[0][row])
        return 0

    lax.fori_loop(0, lines // 24, piece, 0)


def states_kernel(chips, from_ref, to_ref, own_ref, other_ref, *refs):
    me = lax.axis_index("yz")
    core, from_base, to_base = me % 2, me * (18 * (chips - 1)), me * 36
    arrived, (mine_ref, theirs_ref) = refs[: chips - 1], refs[chips - 1 :]
    lines = own_ref.shape[1]

    def piece(at, _):
        span = pl.ds(pl.multiple_of(at * 24, 8), 24)
        for side in range(2):
            into = [jnp.zeros((24, own_ref.shape[2]), F32) for _ in range(3)]
            for at_chip in range(chips - 1):
                for k in range(3):
                    value = arrived[at_chip][k, span, :]
                    for row in range(3):
                        into[row] += from_ref[from_base + (9 * (side * (chips - 1) + at_chip) + 3 * row + k)] * value
            for_mine = (core == 0) if side == 0 else (core == 1)
            for row in range(3):
                to_mine = sum(to_ref[to_base + (18 * side + 3 * row + k)] * into[k] for k in range(3))
                to_theirs = sum(to_ref[to_base + (18 * side + 9 + 3 * row + k)] * into[k] for k in range(3))
                near = 3 * side + row
                mine_ref[near, span, :] = to_mine + jnp.where(for_mine, other_ref[near, span, :], 0.0)
                theirs_ref[near, span, :] = to_theirs + jnp.where(
                    for_mine, 0.0, own_ref[near, span, :]
                )
        return 0

    lax.fori_loop(0, lines // 24, piece, 0)


def span_kernel(smooth_ref, mixed_ref, x_ref, smooth_out, mixed_out):
    fields, pair, span, cells = x_ref.shape
    wide = jnp.concatenate([x_ref[:, row].reshape(fields * span, cells) for row in range(pair)], 1)
    mixed = dot(mixed_ref[...], stacked(padded(wide, mixed_ref.shape[1] // 3)))
    for field in range(fields):
        part = slice(field * span, (field + 1) * span)
        smooth = dot(smooth_ref[...], stacked(wide[part]))
        for row in range(pair):
            place = slice(row * cells, (row + 1) * cells)
            smooth_out[field, row] = smooth[:, place]
            mixed_out[field, row] = mixed[part, place]


def rates_kernel(last_ref, logs_ref, sums_ref, ends_ref, fwd_ref, bwd_ref, *outs):
    win_ref, rf_ref, wout_ref, rb_ref, carry_ref, tail_ref, gains_ref = outs
    rows, span, cells = fwd_ref.shape

    def gathered(rate, mat):
        value = jnp.log(rate)
        high = value.astype(BF16)
        rest = value - high.astype(F32)
        middle = rest.astype(BF16)
        low = (rest - middle.astype(F32)).astype(BF16)
        terms = jnp.concatenate([high, middle, low], axis=1)
        both = dot(terms, mat)
        return both[:, :cells], both[:, cells:], terms

    def across(which, terms):
        mat = ends_ref[which][:, : terms.shape[1]]
        return [lax.dot_general(mat, terms[row * span : (row + 1) * span], (((1,), (1,)), ((), ())),
                                preferred_element_type=F32) for row in range(rows)]

    fwd = fwd_ref[...].reshape(rows * span, cells)
    bwd = bwd_ref[...].reshape(rows * span, cells)
    lane = lax.broadcasted_iota(jnp.int32, fwd.shape, 1)
    relative, absolute, terms = gathered(fwd, logs_ref[0])
    fwd_ends = across(0, terms)
    win_ref[...] = ((1.0 - fwd) * jnp.exp(-relative)).reshape(rows, span, cells)
    rf_ref[...] = jnp.exp(relative).reshape(rows, span, cells)
    entered = jnp.exp(absolute)
    relative, absolute, terms = gathered(bwd, logs_ref[1])
    bwd_ends = across(1, terms)
    grow = jnp.exp(relative)
    keep = jnp.where((lane == cells - 1) & (last_ref[0] == 1), 1.0, 1.0 - bwd)
    weight = keep * jnp.exp(-relative)
    wout_ref[...] = weight.reshape(rows, span, cells)
    rb_ref[...] = grow.reshape(rows, span, cells)
    tail_ref[...] = jnp.exp(absolute).reshape(rows, span, cells)
    high, low = parted(entered * weight)
    terms = jnp.concatenate([high, low], axis=1)
    carry_ref[...] = (grow * dot(terms, sums_ref[...])).reshape(rows, span, cells)
    carry_ends = across(2, terms)
    gains_ref[...] = jnp.zeros_like(gains_ref)
    for row in range(rows):
        ends_f, ends_b = jnp.exp(fwd_ends[row]), jnp.exp(bwd_ends[row])
        gains = (ends_f[0:1], ends_b[0:1], carry_ends[row][0:1] * ends_b[1:2], ends_f[1:2],
                 ends_b[1:2])
        for at, gain in enumerate(gains):
            gains_ref[at, row, :, :span] = gain


def sweep_kernel(rows, smooth_ref, mixed_ref, wall_ref, sums_ref, mine_ref,
                 recv_ref, u_ref, w_ref, win_ref, rf_ref, wout_ref, rb_ref, out_ref, last_ref,
                 first_ref, us_ref, ws_ref):
    tile = u_ref.shape[1]
    cells = u_ref.shape[2]
    fields, half = mine_ref.shape[1], mine_ref.shape[2]
    span = 2 * half
    lines = fields * rows
    at = pl.program_id(0)

    @pl.when(at == 0)
    def _():
        us_ref[pl.ds(6 * fields * span, us_ref.shape[0] - 6 * fields * span), :] = jnp.zeros(
            (us_ref.shape[0] - 6 * fields * span, cells), F32)
        ws_ref[pl.ds(2 * fields * span, ws_ref.shape[0] - 2 * fields * span), :] = jnp.zeros(
            (ws_ref.shape[0] - 2 * fields * span, cells), F32)
        last_ref[...] = jnp.zeros_like(last_ref)
        first_ref[...] = jnp.zeros_like(first_ref)
        first_core = lax.axis_index("yz") % 2 == 0

        def state(k):
            mine, recv = mine_ref[k], recv_ref[k]
            both = [jnp.where(first_core, mine, recv), jnp.where(first_core, recv, mine)]
            return jnp.concatenate(both, axis=1).reshape(fields * span, cells)

        for pair in ((0, 3), (1, 2), (4, 5)):
            wide = jnp.concatenate([state(k) for k in pair], axis=1)
            for field in range(fields):
                part = slice(field * span, (field + 1) * span)
                smooth = dot(smooth_ref[...], stacked(wide[part]))
                for place, k in enumerate(pair):
                    us_ref[pl.ds((k * fields + field) * span, span), :] = smooth[
                        :, place * cells : (place + 1) * cells
                    ]
            if pair == (0, 3):
                mixed = dot(mixed_ref[...], stacked(padded(wide, mixed_ref.shape[1] // 3)))
                for place in range(2):
                    ws_ref[pl.ds(place * fields * span, fields * span), :] = mixed[
                        :, place * cells : (place + 1) * cells
                    ]

    u_flat = u_ref.reshape(lines * tile, cells)
    w_flat = w_ref.reshape(lines * tile, cells)
    out_flat = out_ref.reshape(lines * tile, cells)
    rate_flat = [ref.reshape(rows * tile, cells) for ref in (win_ref, rf_ref, wout_ref, rb_ref)]
    lane = lax.broadcasted_iota(jnp.int32, (lines, last_ref.shape[1]), 1)
    last, first = last_ref[...], first_ref[...]
    rates = [
        jnp.concatenate([
            value for z in range(tile) for value in [ref[pl.ds(z, rows, stride=tile), :]] * fields], 0)
        for ref in rate_flat
    ]
    rights = []
    for z in range(0, tile, 2):
        wide = []
        for zz in (z, z + 1):
            where = at * tile + zz
            wide.append(jnp.concatenate([
                u_flat[pl.ds(zz, lines, stride=tile), :],
                us_ref[pl.ds(where, us_ref.shape[0] // span, stride=span), :],
                w_flat[pl.ds(zz, lines, stride=tile), :],
                ws_ref[pl.ds(where, ws_ref.shape[0] // span, stride=span), :]], 0))
        right = dot(wall_ref[...], stacked(jnp.concatenate(wide, 1)))
        rights += [right[:, :cells], right[:, cells:]]
    ahead = running(jnp.concatenate(rights, 0) * rates[0], sums_ref[0])
    ahead, total = ahead[:, :cells] * rates[1], ahead[:, cells:]
    result = running(ahead * rates[2], sums_ref[1])
    result, total_back = result[:, :cells] * rates[3], result[:, cells:]
    for z in range(tile):
        part = slice(z * lines, (z + 1) * lines)
        here = lane == at * tile + z
        out_flat[pl.ds(z, lines, stride=tile), :] = result[part]
        last = jnp.where(here, total[part], last)
        first = jnp.where(here, total_back[part], first)
    last_ref[...] = last
    first_ref[...] = first


def close_kernel(carry_ref, tail_ref, enter_ref, back_ref, t_ref, out_ref):
    fields, rows, span, _ = t_ref.shape
    for field in range(fields):
        enter = enter_ref[field].T[:span]
        back = back_ref[field].T[:span]
        for row in range(rows):
            out_ref[field, row] = (
                t_ref[field, row]
                + carry_ref[row] * enter[:, row : row + 1]
                + tail_ref[row] * back[:, row : row + 1]
            )


def params(limit):
    return pltpu.CompilerParams(vmem_limit_bytes=limit * 2**20)


def cost(flops, moved):
    return pl.CostEstimate(flops=int(flops), bytes_accessed=int(moved), transcendentals=0)


def whole(memory=pltpu.VMEM):
    return pl.BlockSpec(memory_space=memory)


SMEM = whole(pltpu.SMEM)


def shards(fields, inflow, rates_fwd, rates_bwd, flux_wall, flux_span, viscosity):
    n_fields, rows, span, cells = fields.shape
    devs, sections = lax.axis_size("yz"), lax.axis_size("gx")
    me, section = lax.axis_index("yz"), lax.axis_index("gx")
    chips, half = devs // 2, span // 2
    lines = n_fields * rows
    taps, local, reach, *maps = wall_tables(rows * devs, devs)
    flat = lambda table: jnp.asarray(np.asarray(table, np.float32).reshape(-1))
    taps, chip_mix, from_chip, to_core = (flat(table) for table in (taps, *maps))
    f32 = lambda table: jnp.asarray(np.asarray(table, np.float32))
    span_ops = operators(span, True)
    wall_ops, wall_plain, wall_pick, n_us, n_ws = wall_layout(local, reach, n_fields)
    width = wall_pick.shape[1]
    span_width = -(-n_fields * span // 128) * 128
    pad = lambda mat: np.pad(mat, [(0, 0)] * (mat.ndim - 1) + [(0, span_width - n_fields * span)])
    size = 8
    pick_rows = lambda count: np.pad(
        np.repeat(np.eye(n_fields), count, axis=0), ((0, 0), (0, size - n_fields)))
    span_cols = np.pad(pad(np.repeat(np.eye(n_fields), span, axis=1)), ((0, size - n_fields), (0, 0)))
    wall_cols = np.pad(wall_pick, ((0, size - n_fields), (0, 0)))
    square = lambda mat: jnp.pad(mat, ((0, size - n_fields), (0, size - n_fields)))
    smooth_mat = jnp.asarray(split(span_ops[0]))
    dev_block = lambda *shape: pl.BlockSpec(
        (1, *shape), lambda i, dev: (dev[0],) + (0,) * len(shape))
    full_block = lambda *shape: pl.BlockSpec(shape, lambda i, dev: (0,) * len(shape))
    all_span = n_fields * span
    wall_mat, mixed_mat = pl.pallas_call(
        functools.partial(mats_kernel_at, n_fields),
        grid_spec=pltpu.PrefetchScalarGridSpec(
            num_scalar_prefetch=1,
            grid=(1,),
            in_specs=[
                full_block(size, size), full_block(size, size), full_block(1, size),
                full_block(lines, size), full_block(size, width), dev_block(2, lines, width),
                dev_block(lines, width), full_block(all_span, size), full_block(size, span_width),
                full_block(2, all_span, span_width), full_block(all_span, span_width)],
            out_specs=[full_block(lines, 3 * width), full_block(all_span, 3 * span_width)],
        ),
        out_shape=[
            jax.ShapeDtypeStruct((lines, 3 * width), BF16),
            jax.ShapeDtypeStruct((all_span, 3 * span_width), BF16)],
        compiler_params=params(LIMITS["mats"]),
        cost_estimate=cost(10**7, 8 * 10**6),
        name="mats",
    )(me.astype(jnp.int32).reshape(1), square(flux_wall), square(flux_span),
      jnp.pad(viscosity, (0, size - n_fields)).reshape(1, size), f32(pick_rows(rows)),
      f32(wall_cols), f32(wall_ops), f32(wall_plain), f32(pick_rows(span)), f32(span_cols),
      f32(np.stack([pad(np.tile(op, (n_fields, n_fields))) for op in span_ops[1:]])),
      f32(pad(np.kron(np.eye(n_fields), span_ops[0]))))
    tri = np.triu(np.ones((cells, cells), np.float32))
    ones = np.ones_like(tri)
    twice = lambda mat: np.concatenate([mat, mat], 0)
    sums = jnp.asarray(np.stack([
        twice(np.concatenate([tri, ones], 1)), twice(np.concatenate([tri.T, ones], 1))
    ])).astype(BF16)
    logs_fwd = tri - tri[:, cells // 2 - 1 :][:, :1]
    logs_bwd = tri.T - tri.T[:, cells // 2 :][:, :1]
    thrice = lambda mat: np.concatenate([mat, mat, mat], 0)
    logs = jnp.asarray(np.stack([
        thrice(np.concatenate([logs_fwd, tri], 1)), thrice(np.concatenate([logs_bwd, tri.T], 1))
    ])).astype(BF16)

    tap_shape = jax.ShapeDtypeStruct((6, n_fields, half, cells), F32)
    tap_block = pl.BlockSpec((6, 1, half, cells), lambda f: (0, f, 0, 0))
    keep, send = pl.pallas_call(
        taps_kernel,
        grid=(n_fields,),
        in_specs=[SMEM, pl.BlockSpec((1, rows, span, cells), lambda f: (f, 0, 0, 0))],
        out_specs=[tap_block, tap_block],
        out_shape=[tap_shape, tap_shape],
        compiler_params=params(LIMITS["taps"]),
        cost_estimate=cost(12 * fields.size, 4 * fields.size),
        name="taps",
    )(taps, fields)
    swap_cores = [(dev, dev ^ 1) for dev in range(devs)]
    tap_lines = n_fields * half
    keep = keep.reshape(6, tap_lines, cells)
    other = lax.ppermute(send.reshape(6, tap_lines, cells), "yz", swap_cores)
    part_shape = jax.ShapeDtypeStruct((3, tap_lines, cells), F32)
    outgoing = pl.pallas_call(
        functools.partial(chip_kernel, chips),
        in_specs=[SMEM, whole(), whole()],
        out_specs=[whole()] * (chips - 1),
        out_shape=[part_shape] * (chips - 1),
        compiler_params=params(LIMITS["chip"]),
        cost_estimate=cost(6 * keep.size, 12 * keep.size),
        name="chip",
    )(chip_mix, keep, other)
    held_fields, held_fwd, held_bwd, wall_mat, mixed_mat, *outgoing = lax.optimization_barrier(
        (fields, rates_fwd, rates_bwd, wall_mat, mixed_mat, *outgoing))
    arrived = [
        lax.ppermute(value, "yz", [(dev, dev ^ (2 * (at + 1))) for dev in range(devs)])
        for at, value in enumerate(outgoing)
    ]
    pair_block = pl.BlockSpec((n_fields, 2, span, cells), lambda i: (0, i, 0, 0))
    field_shape = jax.ShapeDtypeStruct(fields.shape, F32)
    smooth, mixed = pl.pallas_call(
        span_kernel,
        grid=(rows // 2,),
        in_specs=[whole(), whole(), pair_block],
        out_specs=[pair_block, pair_block],
        out_shape=[pltpu.HBM(fields.shape, F32)] * 2,
        compiler_params=params(LIMITS["span"]),
        cost_estimate=cost(2 * 4000 * fields.size, 12 * fields.size),
        name="span",
    )(smooth_mat, mixed_mat, held_fields)

    n_rate = 4
    rate_block = pl.BlockSpec((n_rate, span, cells), lambda i: (i, 0, 0))
    rate_shape = jax.ShapeDtypeStruct(rates_fwd.shape, F32)
    is_last = (section == sections - 1).astype(jnp.int32).reshape(1)
    lanes = -(-span // 128) * 128
    widen = lambda value: jnp.pad(value, [(0, 0)] * (value.ndim - 1) + [(0, lanes - span)])
    ends = np.zeros((3, 16, 3 * cells))
    ends[:, 0] = 1.0
    ends[0, 1] = np.tile(np.arange(cells) >= cells // 2, 3)
    ends[1, 1] = np.tile(np.arange(cells) < cells // 2, 3)
    *rate_parts, carry, tail, gains = pl.pallas_call(
        rates_kernel,
        grid=(rows // n_rate,),
        in_specs=[SMEM, whole(), whole(), whole(), rate_block, rate_block],
        out_specs=[rate_block] * 6 + [pl.BlockSpec((5, n_rate, 1, lanes), lambda i: (0, i, 0, 0))],
        out_shape=[pltpu.HBM(rates_fwd.shape, F32)] * 6 + [jax.ShapeDtypeStruct((5, rows, 1, lanes), F32)],
        compiler_params=params(LIMITS["rates"]),
        cost_estimate=cost(2 * 4000 * rates_fwd.size, 32 * rates_fwd.size),
        name="rates",
    )(is_last, logs, sums[1, :, :cells], jnp.asarray(ends.astype(BF16)), held_fwd, held_bwd)
    smooth, mixed, gains, *arrived = lax.optimization_barrier((smooth, mixed, gains, *arrived))
    six_shape = jax.ShapeDtypeStruct((6, tap_lines, cells), F32)
    mine, theirs = pl.pallas_call(
        functools.partial(states_kernel, chips),
        in_specs=[SMEM] * 2 + [whole()] * (chips + 1),
        out_specs=[whole()] * 2,
        out_shape=[six_shape] * 2,
        compiler_params=params(LIMITS["states"]),
        cost_estimate=cost(20 * keep.size, 20 * keep.size),
        name="states",
    )(from_chip, to_core, keep, other, *arrived)
    recv = lax.ppermute(theirs, "yz", swap_cores)
    recv, gains = lax.optimization_barrier((recv, gains.reshape(5, rows, lanes)))
    end_fwd, end_bwd = gains[3], gains[4]
    gains = gains[:3]
    others = [
        lax.ppermute(gains, "gx", [(at, (at + hop) % sections) for at in range(sections)])
        for hop in range(1, sections)
    ]
    arrivals = jnp.stack([gains] + others)
    every = jnp.stack([
        lax.dynamic_index_in_dim(arrivals, (section - at) % sections, 0, False)
        for at in range(sections)
    ])
    gain_f, gain_b, gain_c = every[:, 0], every[:, 1], every[:, 2]
    turned = [None] * sections
    turned[sections - 1] = jnp.zeros_like(gain_f[0])
    for at in range(sections - 2, -1, -1):
        turned[at] = gain_c[at + 1] + gain_b[at + 1] * gain_f[at + 1] * turned[at + 1]
    own = lambda value: lax.dynamic_index_in_dim(value, section, 0, False)
    turn = own(jnp.stack(turned))
    turn_out = own(gain_b) * turn
    start_gain, hop_fwd, hop_bwd = [], [], []
    one, zero = jnp.ones_like(gain_f[0]), jnp.zeros_like(gain_f[0])
    for to in range(sections):
        value = one
        for at in range(to):
            value = value * gain_f[at]
        start_gain.append(value)
        fwd_row, bwd_row = [], []
        for hop in range(1, sections):
            source = (to - hop) % sections
            value = one
            for at in range(min(source, to) + 1, max(source, to)):
                value = value * (gain_f if source < to else gain_b)[at]
            fwd_row.append(value if source < to else zero)
            bwd_row.append(value if source > to else zero)
        hop_fwd.append(jnp.stack(fwd_row))
        hop_bwd.append(jnp.stack(bwd_row))
    entering = own(jnp.stack(start_gain))[None] * widen(inflow)
    hop_fwd, hop_bwd = own(jnp.stack(hop_fwd)), own(jnp.stack(hop_bwd))
    own_gain = own(gain_f)

    tile = 8
    line_block = pl.BlockSpec((lines, tile, cells), lambda i: (0, i, 0))
    rate_tile = pl.BlockSpec((rows, tile, cells), lambda i: (0, i, 0))
    end_block = pl.BlockSpec((lines, lanes), lambda i: (0, 0))
    end_shape = jax.ShapeDtypeStruct((lines, lanes), F32)
    as_lines = lambda value: value.reshape(lines, span, cells)
    as_states = lambda value: value.reshape(6, n_fields, half, cells)
    swept, last, first = pl.pallas_call(
        functools.partial(sweep_kernel, rows),
        grid=(span // tile,),
        in_specs=[whole()] * 6 + [line_block] * 2 + [rate_tile] * 4,
        out_specs=[line_block, end_block, end_block],
        out_shape=[jax.ShapeDtypeStruct((lines, span, cells), F32), end_shape, end_shape],
        scratch_shapes=[
            pltpu.VMEM((n_us * span, cells), F32), pltpu.VMEM((n_ws * span, cells), F32)],
        compiler_params=params(LIMITS["sweep"]),
        cost_estimate=cost(2 * 3000 * fields.size, 12 * fields.size),
        name="sweep",
    )(smooth_mat, mixed_mat, wall_mat, sums, as_states(mine), as_states(recv),
      as_lines(smooth), as_lines(mixed), *rate_parts)
    last = last.reshape(n_fields, rows, lanes) * end_fwd[None]
    first = first.reshape(n_fields, rows, lanes) * end_bwd[None]

    upstream = first + turn_out[None] * last
    back = jnp.zeros_like(last)
    for hop in range(1, sections):
        payload = jnp.where(section + hop < sections, last, upstream)
        got = lax.ppermute(payload, "gx", [(at, (at + hop) % sections) for at in range(sections)])
        entering = entering + hop_fwd[hop - 1][None] * got
        back = back + hop_bwd[hop - 1][None] * got
    back = back + turn[None] * (own_gain[None] * entering + last)

    n_close = 8
    close_block = pl.BlockSpec((n_fields, n_close, span, cells), lambda i: (0, i, 0, 0))
    gain_block = pl.BlockSpec((n_close, span, cells), lambda i: (i, 0, 0))
    state_block = pl.BlockSpec((n_fields, n_close, lanes), lambda i: (0, i, 0))
    return pl.pallas_call(
        close_kernel,
        grid=(rows // n_close,),
        in_specs=[gain_block, gain_block, state_block, state_block, close_block],
        out_specs=close_block,
        out_shape=field_shape,
        compiler_params=params(LIMITS["close"]),
        cost_estimate=cost(4 * fields.size, 10 * fields.size),
        name="close",
    )(carry, tail, entering, back, swept.reshape(fields.shape))


def solution(mesh):
    placed = (
        P(None, "yz", None, "gx"), P(None, "yz", None), P("yz", None, "gx"), P("yz", None, "gx"),
        P(), P(), P(),
    )
    return jax.shard_map(
        shards, mesh=mesh, in_specs=placed, out_specs=P(None, "yz", None, "gx"), check_vma=False
    )
```

time: 1780 us -> 104 us (0.06); the launches traced: 1750 us -> 103 us
  local copies, waits for them, and re-layouts: 1330 us -> 5.88 us
  other arithmetic: 214 us -> 0.98 us
  matrix products: 130 us -> 0 us
  Pallas kernels: 0 us -> 73.3 us
  blocking collectives: 58.9 us -> 0 us
    slice x91 -> x0, local copies, waits for them, and re-layouts: 649 us -> none  [the longest x47 360 us: shards(): lax.associative_scan(compose, (bwd_rate, (1.0 - bwd_rate) * forward), rev...]
    pad x48 -> x2, local copies, waits for them, and re-layouts: 394 us -> 1.19 us  [shards(): jnp.pad(mat, ((0, size - n_fields), (0, size - n_fields)))]
    dot_general x13 -> x0, matrix products: 130 us -> none  [the longest x1 42 us: shards(): stacked = jnp.einsum('kab,fbzx->kfazx', wall_ops, smooth, precision=highest)]
    add x57 -> x2, other arithmetic: 115 us -> 0.76 us  [the longest x1 0.73 us: shards(): back = back + turn[None] * (own_gain[None] * entering + last)]
    pallas_call x0 -> x8, Pallas kernels: none -> 73.3 us  [the longest x1 23.6 us: shards(): pl.pallas_call(functools.partial(sweep_kernel, rows), grid=(span // tile,...]
    rev x4 -> x0, local copies, waits for them, and re-layouts: 63.3 us -> none  [the longest x2 62.6 us: shards(): lax.associative_scan(compose, (bwd_rate, (1.0 - bwd_rate) * forward), rev...]
    mul x24 -> x2, local copies, waits for them, and re-layouts: 61.5 us -> 0.01 us  [the longest x1 0.01 us: shards(): back = back + hop_bwd[hop - 1][None] * got]
    all_gather x4 -> x0, blocking collectives: 58.9 us -> none  [prefix(): pieces = jax.tree.map(lambda part: lax.all_gather(part, axis), value)]
  transfers between devices with their start and end apart: 3 -> 11, of which waited for: 0 -> 3; matrix products, arithmetic and copies ran while one was open for 55% -> 2% of each run, Pallas kernels for 0% -> 50%
where the time goes in v1:
time: 104 us; the launch traced here: 103 us
  Pallas kernels  73.3 us (70%)
  starting transfers between devices  13.7 us (13%)
  waiting for transfers between devices  9.34 us (9%)
  local copies, waits for them, and re-layouts  5.88 us (6%)
    pallas_call x1, Pallas kernels, shards(): pl.pallas_call(functools.partial(sweep_kernel, rows), grid=(span // tile,...  23.6 us
    pallas_call x1, Pallas kernels, shards(): pl.pallas_call(span_kernel, grid=(rows // 2,), in_specs=[whole(), whole()...  14.3 us
    pallas_call x1, Pallas kernels, shards(): pl.pallas_call(close_kernel, grid=(rows // n_close,), in_specs=[gain_bloc...  10.2 us
    pallas_call x1, Pallas kernels, shards(): pl.pallas_call(taps_kernel, grid=(n_fields,), in_specs=[SMEM, pl.BlockSpe...  7.51 us
    pallas_call x1, Pallas kernels, shards(): pl.pallas_call(rates_kernel, grid=(rows // n_rate,), in_specs=[SMEM, whol...  7.25 us
    ppermute x3, waiting for transfers between devices, shards(): lax.ppermute(payload, 'gx', [(at, (at + hop) % sections) for at in range(...  7.11 us
    pallas_call x1, Pallas kernels, shards(): pl.pallas_call(functools.partial(mats_kernel_at, n_fields), grid_spec=plt...  6.89 us
    ppermute x3, starting transfers between devices, shards(): lax.ppermute(gains, 'gx', [(at, (at + hop) % sections) for at in range(se...  5.13 us
  transfers between devices with their start and end apart: 11, of which 3 were waited for; matrix products, arithmetic and copies ran while one was open for 2% of the time, Pallas kernels for 50%

profile of v1, /device:TPU:0, one launch (start us, length us, event | category | flops | bytes accessed | tf_op | source)
XLA Modules:
  0.0 103.5 jit_solution(1648232373229190812)
XLA Ops:
  0.0 7.5 %taps.1 = (f32[6,5,48,128]{3,2,1,0:T(8,128)}, f32[6,5,48,128]{3,2,1,0:T(8,128)}) custom-call(f32[1536]{0:T(1024)} %constant.114.clone.taps_ref, f32[5,32,96,128]{3,2,1,0:T(8,128)} %x_ref.2), custom_call_target="tpu_custom_call" | custom-call | flops 23592960 | bytes 7864320 | tf_op jit(solution)/shard_map/taps/pallas_call | solution.py:495
  7.5 0.4 collective-permute-start
  7.9 0.6 pad.15.refs_0_
  8.5 0.6 pad.16.refs_1_
  9.1 0.6 pad_bitcast_fusion.refs_2_
  9.7 6.9 %mats.1 = (bf16[160,1152]{1,0:T(8,128)(2,1)}, bf16[480,1536]{1,0:T(8,128)(2,1)}) custom-call(s32[1]{0:T(128)} %bitcast.1.dev_ref, f32[8,8]{1,0:T(8,128)} %pad.15.refs_0_, f32[8,8]{1,0:T(8,128)} %pad.16.refs_1_, f32[1,8]{1,0:T(1,128)} %pad_bitcast_fusion.refs_2_, f32[160,8]{1,0:T(8,128)} %constant.119.clone.refs_3_, f32[8,384]{1,0:T(8,128)} %constant.120.clone.refs_4_, ...), custom_call_target="tpu_custom_call" | custom-call | flops 10000000 | bytes 8000000 | tf_op jit(solution)/shard_map/mats/pallas_call | solution.py:457
  16.6 1.1 %copy-done.1 = f32[6,5,48,128]{3,2,1,0:T(8,128)S(1)} copy-done((f32[6,5,48,128]{3,2,1,0:T(8,128)S(1)}, f32[6,5,48,128]{3,2,1,0:T(8,128)}, u32[]{:S(2)}) %copy-start.1) | copy-done | bytes 737304
  17.7 1.6 %chip.1 = (f32[3,240,128]{2,1,0:T(8,128)S(1)}, f32[3,240,128]{2,1,0:T(8,128)S(1)}, f32[3,240,128]{2,1,0:T(8,128)S(1)}) custom-call(f32[288]{0:T(512)S(1)} %copy-done.5, f32[6,240,128]{2,1,0:T(8,128)S(1)} %bitcast.83, f32[6,240,128]{2,1,0:T(8,128)} %collective-permute-done.other_ref), custom_call_target="tpu_custom_call" | custom-call | flops 1105920 | bytes 2211840 | tf_op jit(solution)/shard_map/chip/pallas_call | solution.py:510
  19.3 2.6 %collective-permute-start.1 = (f32[3,240,128]{2,1,0:T(8,128)S(1)}, f32[3,240,128]{2,1,0:T(8,128)S(1)}, u32[]{:S(2)}, u32[]{:S(2)}) collective-permute-start(f32[3,240,128]{2,1,0:T(8,128)S(1)} %get-tuple-element.58), channel_id=1, source_target_pairs={{0,2},{1,3},{2,0},{3,1},{4,6},{5,7},{6,4},{7,5},{8,10},{9,11},{10,... | collective-permute-start | bytes 1105928 | tf_op jit(solution)/shard_map/ppermute | solution.py:522
  21.9 1.5 %collective-permute-start.2 = (f32[3,240,128]{2,1,0:T(8,128)S(1)}, f32[3,240,128]{2,1,0:T(8,128)S(1)}, u32[]{:S(2)}, u32[]{:S(2)}) collective-permute-start(f32[3,240,128]{2,1,0:T(8,128)S(1)} %get-tuple-element.59), channel_id=1, source_target_pairs={{0,4},{1,5},{2,6},{3,7},{4,0},{5,1},{6,2},{7,3},{8,12},{9,13},{10,... | collective-permute-start | bytes 1105928 | tf_op jit(solution)/shard_map/ppermute | solution.py:522
  23.4 0.0 collective-permute-start.3
  23.4 1.4 %copy-done.8 = bf16[480,1536]{1,0:T(8,128)(2,1)S(1)} copy-done((bf16[480,1536]{1,0:T(8,128)(2,1)S(1)}, bf16[480,1536]{1,0:T(8,128)(2,1)}, u32[]{:S(2)}) %copy-start.8) | copy-done | bytes 1474584
  24.8 14.3 %span.1 = (f32[5,32,96,128]{3,2,1,0:T(8,128)}, f32[5,32,96,128]{3,2,1,0:T(8,128)}) custom-call(bf16[96,288]{1,0:T(8,128)(2,1)S(1)} %copy-done.11, bf16[480,1536]{1,0:T(8,128)(2,1)S(1)} %copy-done.8, f32[5,32,96,128]{3,2,1,0:T(8,128)S(1)} %copy-done), custom_call_target="tpu_custom_call" | custom-call | flops 15728640000 | bytes 23592960 | tf_op jit(solution)/shard_map/span/pallas_call | solution.py:527
  39.1 0.0 copy-start.3
  39.2 0.0 copy-start.4
  39.2 7.2 %rates.1 = (f32[32,96,128]{2,1,0:T(8,128)}, f32[32,96,128]{2,1,0:T(8,128)}, f32[32,96,128]{2,1,0:T(8,128)}, f32[32,96,128]{2,1,0:T(8,128)}, f32[32,96,128]{2,1,0...) custom-call(s32[1]{0:T(128)} %bitcast.last_ref, bf16[2,384,256]{2,1,0:T(8,128)(2,1)S(1)} %copy-done.10, ...), custom_call_target="tpu_custom_call" | custom-call | flops 3145728000 | bytes 12582912 | tf_op jit(solution)/shard_map/rates/pallas_call | solution.py:548
  46.5 2.0 %states.1 = (f32[6,240,128]{2,1,0:T(8,128)S(1)}, f32[6,240,128]{2,1,0:T(8,128)S(1)}) custom-call(f32[432]{0:T(512)S(1)} %copy-done.3, f32[288]{0:T(512)S(1)} %copy-done.4, f32[6,240,128]{2,1,0:T(8,128)S(1)} %bitcast.84, f32[6,240,128]{2,1,0:T(8,128)} %collective-permute-done.other_ref, f32[3,240,128]{2,1,0:T(8,128)S(1)} %collective-permute-done.1.refs_0_, ...), custom_call_target="tpu_custom_call" | custom-call | flops 3686400 | bytes 3686400 | tf_op jit(solution)/shard_map/states/pallas_call | solution.py:560
  48.5 0.9 copy-done.9
  49.4 2.2 %collective-permute-done.4 = f32[6,240,128]{2,1,0:T(8,128)S(1)} collective-permute-done((f32[6,240,128]{2,1,0:T(8,128)S(1)}, f32[6,240,128]{2,1,0:T(8,128)S(1)}, u32[]{:S(2)}, u32[]{:S(2)}) %collective-permute-start.4) | collective-permute-done | bytes 737312 | tf_op jit(solution)/shard_map/ppermute | solution.py:569
  51.6 4.1 %collective-permute-start.7 = (f32[3,32,128]{2,1,0:T(8,128)S(1)}, f32[3,32,128]{2,1,0:T(8,128)S(1)}, u32[]{:S(2)}, u32[]{:S(2)}) collective-permute-start(f32[3,32,128]{2,1,0:T(8,128)S(1)} %get-tuple-element.107), channel_id=1, source_target_pairs={{0,24},{8,0},{16,8},{24,16},{1,25},{9,1},{17,9},{25,17},{2,26},{10... | collective-permute-start | bytes 147464 | tf_op jit(solution)/shard_map/ppermute | solution.py:574
  55.7 1.0 collective-permute-start.5
  56.7 23.6 %sweep.1 = (f32[160,96,128]{2,1,0:T(8,128)}, f32[160,128]{1,0:T(8,128)}, f32[160,128]{1,0:T(8,128)}) custom-call(bf16[96,288]{1,0:T(8,128)(2,1)} %constant.118.clone.smooth_ref, bf16[480,1536]{1,0:T(8,128)(2,1)} %get-tuple-element.53.mixed_ref, bf16[160,1152]{1,0:T(8,128)(2,1)} %get-tuple-element.67.wall_ref, bf16[2,256,256]{2,1,0:T(8,128)(2,1)} %constant.139.sums_ref, ...), custom_call_target="tpu_custom_call" | custom-call | flops 11796480000 | bytes 23592960 | tf_op jit(solution)/shard_map/sweep/pallas_call | solution.py:618
  80.4 0.0 copy-start.18
  80.7 0.6 copy-done.14
  81.2 0.0 copy-done.15
  81.3 2.9 %collective-permute-start.10 = (f32[5,32,128]{2,1,0:T(8,128)S(1)}, f32[5,32,128]{2,1,0:T(8,128)S(1)}, u32[]{:S(2)}, u32[]{:S(2)}) collective-permute-start(f32[5,32,128]{2,1,0:T(8,128)S(1)} %get-tuple-element.95), channel_id=1, source_target_pairs={{0,24},{8,0},{16,8},{24,16},{1,25},{9,1},{17,9},{25,17},{2,26},{10... | collective-permute-start | bytes 245768 | tf_op jit(solution)/shard_map/ppermute | solution.py:638
  84.2 1.1 %collective-permute-start.9 = (f32[5,32,128]{2,1,0:T(8,128)S(1)}, f32[5,32,128]{2,1,0:T(8,128)S(1)}, u32[]{:S(2)}, u32[]{:S(2)}) collective-permute-start(f32[5,32,128]{2,1,0:T(8,128)S(1)} %get-tuple-element.96), channel_id=1, source_target_pairs={{0,16},{8,24},{16,0},{24,8},{1,17},{9,25},{17,1},{25,9},{2,18},{10... | collective-permute-start | bytes 245768 | tf_op jit(solution)/shard_map/ppermute | solution.py:638
  85.4 0.1 fusion.11
  85.5 1.6 %collective-permute-done.10 = f32[5,32,128]{2,1,0:T(8,128)S(1)} collective-permute-done((f32[5,32,128]{2,1,0:T(8,128)S(1)}, f32[5,32,128]{2,1,0:T(8,128)S(1)}, u32[]{:S(2)}, u32[]{:S(2)}) %collective-permute-start.10) | collective-permute-done | bytes 81952 | tf_op jit(solution)/shard_map/ppermute | solution.py:638
  87.1 5.5 %collective-permute-done.9 = f32[5,32,128]{2,1,0:T(8,128)S(1)} collective-permute-done((f32[5,32,128]{2,1,0:T(8,128)S(1)}, f32[5,32,128]{2,1,0:T(8,128)S(1)}, u32[]{:S(2)}, u32[]{:S(2)}) %collective-permute-start.9) | collective-permute-done | bytes 81952 | tf_op jit(solution)/shard_map/ppermute | solution.py:638
  92.6 0.7 multiply_add_fusion
  93.3 10.2 %close.1 = f32[5,32,96,128]{3,2,1,0:T(8,128)} custom-call(f32[32,96,128]{2,1,0:T(8,128)} %get-tuple-element.51.carry_ref, f32[32,96,128]{2,1,0:T(8,128)} %get-tuple-element.52.tail_ref, f32[5,32,128]{2,1,0:T(8,128)} %get-tuple-element.80.enter_ref, f32[5,32,128]{2,1,0:T(8,128)} %get-tuple-element.79.back_ref, f32[5,32,96,128]{3,2,1,0:T(8,128)} %bitcast.88), custom_call_target="tpu_custom_call" | custom-call | flops 7864320 | bytes 19660800 | tf_op jit(solution)/shard_map/close/pallas_call | solution.py:647
  (64 shorter events, 0.4 us)
Async XLA Ops:
  0.0 7.9 %copy-start.19 = (f32[5,5]{1,0:T(8,128)S(1)}, f32[5,5]{1,0:T(8,128)}, u32[]{:S(2)}) copy-start(f32[5,5]{1,0:T(8,128)} %param.27) | copy-start | bytes 304
  0.0 8.5 %copy-start.20 = (f32[5,5]{1,0:T(8,128)S(1)}, f32[5,5]{1,0:T(8,128)}, u32[]{:S(2)}) copy-start(f32[5,5]{1,0:T(8,128)} %param.28) | copy-start | bytes 304
  0.0 9.1 %copy-start.22 = (f32[5]{0:T(128)S(1)}, f32[5]{0:T(128)}, u32[]{:S(2)}) copy-start(f32[5]{0:T(128)} %param.29) | copy-start | bytes 64
  7.5 9.0 %collective-permute-start = (f32[6,240,128]{2,1,0:T(8,128)}, f32[6,240,128]{2,1,0:T(8,128)}, u32[]{:S(2)}, u32[]{:S(2)}) collective-permute-start(f32[6,240,128]{2,1,0:T(8,128)} %bitcast.97), channel_id=1, source_target_pairs={{0,1},{1,0},{2,3},{3,2},{4,5},{5,4},{6,7},{7,6},{8,9},{9,8},{10,11... | collective-permute-start | bytes 2211848 | tf_op jit(solution)/shard_map/ppermute | solution.py:508
  9.7 6.9 %copy-start.5 = (f32[288]{0:T(512)S(1)}, f32[288]{0:T(512)}, u32[]{:S(2)}) copy-start(f32[288]{0:T(512)} %constant.115.clone.mix_ref) | copy-start | bytes 3460
  9.7 13.8 %copy-start = (f32[5,32,96,128]{3,2,1,0:T(8,128)S(1)}, f32[5,32,96,128]{3,2,1,0:T(8,128)}, u32[]{:S(2)}) copy-start(f32[5,32,96,128]{3,2,1,0:T(8,128)} %x_ref.2) | copy-start | bytes 23592964
  9.7 13.8 %copy-start.11 = (bf16[96,288]{1,0:T(8,128)(2,1)S(1)}, bf16[96,288]{1,0:T(8,128)(2,1)}, u32[]{:S(2)}) copy-start(bf16[96,288]{1,0:T(8,128)(2,1)} %constant.118.clone.smooth_ref) | copy-start | bytes 165892
  16.6 1.1 %copy-start.1 = (f32[6,5,48,128]{3,2,1,0:T(8,128)S(1)}, f32[6,5,48,128]{3,2,1,0:T(8,128)}, u32[]{:S(2)}) copy-start(f32[6,5,48,128]{3,2,1,0:T(8,128)} %get-tuple-element.44) | copy-start | bytes 2211844
  19.3 19.9 %copy-start.6 = (f32[32,96,128]{2,1,0:T(8,128)S(1)}, f32[32,96,128]{2,1,0:T(8,128)}, u32[]{:S(2)}) copy-start(f32[32,96,128]{2,1,0:T(8,128)} %fwd_ref) | copy-start | bytes 4718596
  19.3 19.8 %copy-start.7 = (f32[32,96,128]{2,1,0:T(8,128)S(1)}, f32[32,96,128]{2,1,0:T(8,128)}, u32[]{:S(2)}) copy-start(f32[32,96,128]{2,1,0:T(8,128)} %bwd_ref) | copy-start | bytes 4718596
  19.3 27.1 %collective-permute-start.1 = (f32[3,240,128]{2,1,0:T(8,128)S(1)}, f32[3,240,128]{2,1,0:T(8,128)S(1)}, u32[]{:S(2)}, u32[]{:S(2)}) collective-permute-start(f32[3,240,128]{2,1,0:T(8,128)S(1)} %get-tuple-element.58), channel_id=1, source_target_pairs={{0,2},{1,3},{2,0},{3,1},{4,6},{5,7},{6,4},{7,5},{8,10},{9,11},{10,... | collective-permute-start | bytes 1105928 | tf_op jit(solution)/shard_map/ppermute | solution.py:522
  21.9 24.5 %collective-permute-start.2 = (f32[3,240,128]{2,1,0:T(8,128)S(1)}, f32[3,240,128]{2,1,0:T(8,128)S(1)}, u32[]{:S(2)}, u32[]{:S(2)}) collective-permute-start(f32[3,240,128]{2,1,0:T(8,128)S(1)} %get-tuple-element.59), channel_id=1, source_target_pairs={{0,4},{1,5},{2,6},{3,7},{4,0},{5,1},{6,2},{7,3},{8,12},{9,13},{10,... | collective-permute-start | bytes 1105928 | tf_op jit(solution)/shard_map/ppermute | solution.py:522
  23.4 23.0 %collective-permute-start.3 = (f32[3,240,128]{2,1,0:T(8,128)S(1)}, f32[3,240,128]{2,1,0:T(8,128)S(1)}, u32[]{:S(2)}, u32[]{:S(2)}) collective-permute-start(f32[3,240,128]{2,1,0:T(8,128)S(1)} %get-tuple-element.60), channel_id=1, source_target_pairs={{0,6},{1,7},{2,4},{3,5},{4,2},{5,3},{6,0},{7,1},{8,14},{9,15},{10,... | collective-permute-start | bytes 1105928 | tf_op jit(solution)/shard_map/ppermute | solution.py:522
  23.4 1.4 %copy-start.8 = (bf16[480,1536]{1,0:T(8,128)(2,1)S(1)}, bf16[480,1536]{1,0:T(8,128)(2,1)}, u32[]{:S(2)}) copy-start(bf16[480,1536]{1,0:T(8,128)(2,1)} %get-tuple-element.53.mixed_ref) | copy-start | bytes 4423684
  24.8 14.3 %copy-start.10 = (bf16[2,384,256]{2,1,0:T(8,128)(2,1)S(1)}, bf16[2,384,256]{2,1,0:T(8,128)(2,1)}, u32[]{:S(2)}) copy-start(bf16[2,384,256]{2,1,0:T(8,128)(2,1)} %constant.138.logs_ref) | copy-start | bytes 1179652
  24.8 14.3 %copy-start.12 = (bf16[256,128]{1,0:T(8,128)(2,1)S(1)}, bf16[256,128]{1,0:T(8,128)(2,1)}, u32[]{:S(2)}) copy-start(bf16[256,128]{1,0:T(8,128)(2,1)} %constant.141.sums_ref) | copy-start | bytes 196612
  24.8 14.3 %copy-start.13 = (bf16[3,16,384]{2,1,0:T(8,128)(2,1)S(1)}, bf16[3,16,384]{2,1,0:T(8,128)(2,1)}, u32[]{:S(2)}) copy-start(bf16[3,16,384]{2,1,0:T(8,128)(2,1)} %constant.129.clone.ends_ref) | copy-start | bytes 110596
  39.1 7.3 %copy-start.2 = (f32[6,5,48,128]{3,2,1,0:T(8,128)S(1)}, f32[6,5,48,128]{3,2,1,0:T(8,128)}, u32[]{:S(2)}) copy-start(f32[6,5,48,128]{3,2,1,0:T(8,128)} %get-tuple-element.44) | copy-start | bytes 2211844
  39.1 7.3 %copy-start.3 = (f32[432]{0:T(512)S(1)}, f32[432]{0:T(512)}, u32[]{:S(2)}) copy-start(f32[432]{0:T(512)} %constant.116.clone.from_ref) | copy-start | bytes 5188
  39.2 7.3 %copy-start.4 = (f32[288]{0:T(512)S(1)}, f32[288]{0:T(512)}, u32[]{:S(2)}) copy-start(f32[288]{0:T(512)} %constant.117.clone.to_ref) | copy-start | bytes 3460
  49.4 2.2 %collective-permute-start.4 = (f32[6,240,128]{2,1,0:T(8,128)S(1)}, f32[6,240,128]{2,1,0:T(8,128)S(1)}, u32[]{:S(2)}, u32[]{:S(2)}) collective-permute-start(f32[6,240,128]{2,1,0:T(8,128)S(1)} %get-tuple-element.64), channel_id=1, source_target_pairs={{0,1},{1,0},{2,3},{3,2},{4,5},{5,4},{6,7},{7,6},{8,9},{9,8},{10,11... | collective-permute-start | bytes 2211848 | tf_op jit(solution)/shard_map/ppermute | solution.py:569
  51.6 5.1 %copy-start.21 = (f32[6,240,128]{2,1,0:T(8,128)}, f32[6,240,128]{2,1,0:T(8,128)S(1)}, u32[]{:S(2)}) copy-start(f32[6,240,128]{2,1,0:T(8,128)S(1)} %collective-permute-done.4) | copy-start | bytes 2211844
  51.6 28.8 %collective-permute-start.7 = (f32[3,32,128]{2,1,0:T(8,128)S(1)}, f32[3,32,128]{2,1,0:T(8,128)S(1)}, u32[]{:S(2)}, u32[]{:S(2)}) collective-permute-start(f32[3,32,128]{2,1,0:T(8,128)S(1)} %get-tuple-element.107), channel_id=1, source_target_pairs={{0,24},{8,0},{16,8},{24,16},{1,25},{9,1},{17,9},{25,17},{2,26},{10... | collective-permute-start | bytes 147464 | tf_op jit(solution)/shard_map/ppermute | solution.py:574
  55.7 24.7 %collective-permute-start.6 = (f32[3,32,128]{2,1,0:T(8,128)S(1)}, f32[3,32,128]{2,1,0:T(8,128)S(1)}, u32[]{:S(2)}, u32[]{:S(2)}) collective-permute-start(f32[3,32,128]{2,1,0:T(8,128)S(1)} %get-tuple-element.107), channel_id=1, source_target_pairs={{0,16},{8,24},{16,0},{24,8},{1,17},{9,25},{17,1},{25,9},{2,18},{10... | collective-permute-start | bytes 147464 | tf_op jit(solution)/shard_map/ppermute | solution.py:574
  55.7 24.7 %collective-permute-start.5 = (f32[3,32,128]{2,1,0:T(8,128)S(1)}, f32[3,32,128]{2,1,0:T(8,128)S(1)}, u32[]{:S(2)}, u32[]{:S(2)}) collective-permute-start(f32[3,32,128]{2,1,0:T(8,128)S(1)} %get-tuple-element.107), channel_id=1, source_target_pairs={{0,8},{8,16},{16,24},{24,0},{1,9},{9,17},{17,25},{25,1},{2,10},{10... | collective-permute-start | bytes 147464 | tf_op jit(solution)/shard_map/ppermute | solution.py:574
  80.4 0.9 copy-start.15
  80.4 5.0 %copy-start.17 = (f32[1,3,32,128]{3,2,1,0:T(8,128)S(1)}, f32[1,3,32,128]{3,2,1,0:T(8,128)}, u32[]{:S(2)}) copy-start(f32[1,3,32,128]{3,2,1,0:T(8,128)} %constant.109.clone.1) | copy-start | bytes 147460
  80.4 5.0 %copy-start.18 = (f32[1,3,32,128]{3,2,1,0:T(8,128)S(1)}, f32[1,3,32,128]{3,2,1,0:T(8,128)}, u32[]{:S(2)}) copy-start(f32[1,3,32,128]{3,2,1,0:T(8,128)} %constant.113.clone.1) | copy-start | bytes 147460
  80.5 12.1 %copy-start.16 = (f32[5,32,96]{2,1,0:T(8,128)S(1)}, f32[5,32,96]{2,1,0:T(8,128)}, u32[]{:S(2)}) copy-start(f32[5,32,96]{2,1,0:T(8,128)} %param.24) | copy-start | bytes 184324
  81.3 5.8 %collective-permute-start.10 = (f32[5,32,128]{2,1,0:T(8,128)S(1)}, f32[5,32,128]{2,1,0:T(8,128)S(1)}, u32[]{:S(2)}, u32[]{:S(2)}) collective-permute-start(f32[5,32,128]{2,1,0:T(8,128)S(1)} %get-tuple-element.95), channel_id=1, source_target_pairs={{0,24},{8,0},{16,8},{24,16},{1,25},{9,1},{17,9},{25,17},{2,26},{10... | collective-permute-start | bytes 245768 | tf_op jit(solution)/shard_map/ppermute | solution.py:638
  84.2 8.4 %collective-permute-start.9 = (f32[5,32,128]{2,1,0:T(8,128)S(1)}, f32[5,32,128]{2,1,0:T(8,128)S(1)}, u32[]{:S(2)}, u32[]{:S(2)}) collective-permute-start(f32[5,32,128]{2,1,0:T(8,128)S(1)} %get-tuple-element.96), channel_id=1, source_target_pairs={{0,16},{8,24},{16,0},{24,8},{1,17},{9,25},{17,1},{25,9},{2,18},{10... | collective-permute-start | bytes 245768 | tf_op jit(solution)/shard_map/ppermute | solution.py:638
  85.3 7.3 %collective-permute-start.8 = (f32[5,32,128]{2,1,0:T(8,128)S(1)}, f32[5,32,128]{2,1,0:T(8,128)S(1)}, u32[]{:S(2)}, u32[]{:S(2)}) collective-permute-start(f32[5,32,128]{2,1,0:T(8,128)S(1)} %get-tuple-element.94), channel_id=1, source_target_pairs={{0,8},{8,16},{16,24},{24,0},{1,9},{9,17},{17,25},{25,1},{2,10},{10... | collective-permute-start | bytes 245768 | tf_op jit(solution)/shard_map/ppermute | solution.py:638
  (2 other events, 1.8 us)

commit v2 on v1

--- a/solution.py
+++ b/solution.py
@@ -10,7 +10,7 @@
 
 F32, BF16 = jnp.float32, jnp.bfloat16
 STEP = 0.5
-LIMITS = {"mats": 56, "taps": 56, "chip": 8, "span": 12, "rates": 12, "states": 10, "sweep": 56, "close": 56}
+LIMITS = {"mats": 56, "taps": 56, "chip": 8, "span": 24, "rates": 24, "states": 10, "sweep": 56, "close": 56}
 
 
 def tridiagonal(points, below, centre, above, periodic):
@@ -125,7 +125,9 @@
     pick = (owner[None] == np.arange(fields)[:, None]).astype(np.float64)
     tall = np.concatenate([parts] * fields, axis=2)
     same = np.repeat(pick, rows, axis=0)
-    return tall[:, 1:], tall[:, 0] * same, pick, us, ws
+    tall[:, 2] *= same
+    tall[:, 0] *= same
+    return tall[:, [1, 2, 0]], pick, us, ws
 
 
 def split(value):
@@ -159,30 +161,27 @@
     return dot(jnp.concatenate([high, low], axis=1), twice)
 
 
-def mats_kernel(fields, flux_wall_ref, flux_span_ref, visc_ref, wall_rows_ref, wall_cols_ref,
-                wall_ref, wall_plain_ref, span_rows_ref, span_cols_ref, span_ref, span_plain_ref,
-                wall_out, span_out):
+def mats_kernel(dev_ref, flux_wall_ref, flux_span_ref, visc_ref, wall_rows_ref, wall_cols_ref,
+                wall_ref, span_rows_ref, span_cols_ref, span_ref, wall_out, span_out):
     exact = functools.partial(jnp.dot, precision=lax.Precision.HIGHEST, preferred_element_type=F32)
-    size = visc_ref.shape[1]
-    here = lax.broadcasted_iota(jnp.int32, (size, size), 0) == lax.broadcasted_iota(
-        jnp.int32, (size, size), 1)
-    visc = jnp.where(here, STEP * visc_ref[...], 0.0)
-    for flux_ref, rows_ref, cols_ref, ops, plain, out in (
-        (flux_wall_ref, wall_rows_ref, wall_cols_ref, wall_ref[0], wall_plain_ref[0], wall_out),
-        (flux_span_ref, span_rows_ref, span_cols_ref, span_ref[...], span_plain_ref[...], span_out),
+    for flux_ref, rows_ref, cols_ref, ops, out in (
+        (flux_wall_ref, wall_rows_ref, wall_cols_ref, wall_ref[0], wall_out),
+        (flux_span_ref, span_rows_ref, span_cols_ref, span_ref[...], span_out),
     ):
-        rows, cols = rows_ref[...], cols_ref[...]
-        first = exact(exact(rows, -STEP * flux_ref[...]), cols)
-        second = exact(exact(rows, visc), cols)
-        high, low = parted(first * ops[0] + second * ops[1] + plain)
+        cols = cols_ref[...]
+        by_field = exact(-STEP * flux_ref[...], cols)
+        parts = []
+        for _ in range(3):
+            part = by_field.astype(BF16)
+            by_field = by_field - part.astype(F32)
+            parts.append(part.astype(F32))
+        mixing = dot(rows_ref[...], jnp.concatenate(parts, axis=0).astype(BF16))
+        visc = exact(STEP * visc_ref[...], cols)[0:1]
+        high, low = parted(mixing * ops[0] + visc * ops[1] + ops[2])
         width = cols.shape[1]
         out[:, :width] = high
         out[:, width : 2 * width] = high
         out[:, 2 * width :] = low
-
-
-def mats_kernel_at(fields, dev_ref, *refs):
-    mats_kernel(fields, *refs)
 
 
 def taps_kernel(taps_ref, x_ref, keep_ref, send_ref):
@@ -439,31 +438,37 @@
     taps, chip_mix, from_chip, to_core = (flat(table) for table in (taps, *maps))
     f32 = lambda table: jnp.asarray(np.asarray(table, np.float32))
     span_ops = operators(span, True)
-    wall_ops, wall_plain, wall_pick, n_us, n_ws = wall_layout(local, reach, n_fields)
+    wall_ops, wall_pick, n_us, n_ws = wall_layout(local, reach, n_fields)
     width = wall_pick.shape[1]
     span_width = -(-n_fields * span // 128) * 128
     pad = lambda mat: np.pad(mat, [(0, 0)] * (mat.ndim - 1) + [(0, span_width - n_fields * span)])
     size = 8
-    pick_rows = lambda count: np.pad(
-        np.repeat(np.eye(n_fields), count, axis=0), ((0, 0), (0, size - n_fields)))
-    span_cols = np.pad(pad(np.repeat(np.eye(n_fields), span, axis=1)), ((0, size - n_fields), (0, 0)))
-    wall_cols = np.pad(wall_pick, ((0, size - n_fields), (0, 0)))
-    square = lambda mat: jnp.pad(mat, ((0, size - n_fields), (0, size - n_fields)))
+    up_to = lambda mat: np.pad(mat, ((0, size - n_fields), (0, 0)))
+    pick_rows = lambda count: jnp.asarray(np.tile(
+        np.pad(np.repeat(np.eye(n_fields), count, axis=0), ((0, 0), (0, size - n_fields))), (1, 3)
+    ).astype(BF16))
+    span_cols = pad(np.repeat(np.eye(n_fields), span, axis=1))
+    tiny = jnp.zeros((3 * size, size), F32)
+    tiny = lax.dynamic_update_slice(tiny, flux_wall, (0, 0))
+    tiny = lax.dynamic_update_slice(tiny, flux_span, (size, 0))
+    tiny = lax.dynamic_update_slice(tiny, viscosity[None], (2 * size, 0))
     smooth_mat = jnp.asarray(split(span_ops[0]))
     dev_block = lambda *shape: pl.BlockSpec(
         (1, *shape), lambda i, dev: (dev[0],) + (0,) * len(shape))
     full_block = lambda *shape: pl.BlockSpec(shape, lambda i, dev: (0,) * len(shape))
     all_span = n_fields * span
     wall_mat, mixed_mat = pl.pallas_call(
-        functools.partial(mats_kernel_at, n_fields),
+        mats_kernel,
         grid_spec=pltpu.PrefetchScalarGridSpec(
             num_scalar_prefetch=1,
             grid=(1,),
             in_specs=[
-                full_block(size, size), full_block(size, size), full_block(1, size),
-                full_block(lines, size), full_block(size, width), dev_block(2, lines, width),
-                dev_block(lines, width), full_block(all_span, size), full_block(size, span_width),
-                full_block(2, all_span, span_width), full_block(all_span, span_width)],
+                pl.BlockSpec((size, size), lambda i, dev: (0, 0)),
+                pl.BlockSpec((size, size), lambda i, dev: (1, 0)),
+                pl.BlockSpec((size, size), lambda i, dev: (2, 0)),
+                full_block(lines, 3 * size), full_block(size, width), dev_block(3, lines, width),
+                full_block(all_span, 3 * size), full_block(size, span_width),
+                full_block(3, all_span, span_width)],
             out_specs=[full_block(lines, 3 * width), full_block(all_span, 3 * span_width)],
         ),
         out_shape=[
@@ -472,11 +477,12 @@
         compiler_params=params(LIMITS["mats"]),
         cost_estimate=cost(10**7, 8 * 10**6),
         name="mats",
-    )(me.astype(jnp.int32).reshape(1), square(flux_wall), square(flux_span),
-      jnp.pad(viscosity, (0, size - n_fields)).reshape(1, size), f32(pick_rows(rows)),
-      f32(wall_cols), f32(wall_ops), f32(wall_plain), f32(pick_rows(span)), f32(span_cols),
-      f32(np.stack([pad(np.tile(op, (n_fields, n_fields))) for op in span_ops[1:]])),
-      f32(pad(np.kron(np.eye(n_fields), span_ops[0]))))
+    )(me.astype(jnp.int32).reshape(1), tiny, tiny, tiny, pick_rows(rows), f32(up_to(wall_pick)),
+      f32(wall_ops), pick_rows(span), f32(up_to(span_cols)),
+      f32(np.stack([
+          pad(np.tile(span_ops[1], (n_fields, n_fields))),
+          pad(np.kron(np.eye(n_fields), span_ops[2])),
+          pad(np.kron(np.eye(n_fields), span_ops[0]))])))
     tri = np.triu(np.ones((cells, cells), np.float32))
     ones = np.ones_like(tri)
     twice = lambda mat: np.concatenate([mat, mat], 0)
@@ -522,11 +528,12 @@
         lax.ppermute(value, "yz", [(dev, dev ^ (2 * (at + 1))) for dev in range(devs)])
         for at, value in enumerate(outgoing)
     ]
-    pair_block = pl.BlockSpec((n_fields, 2, span, cells), lambda i: (0, i, 0, 0))
+    n_span = 4
+    pair_block = pl.BlockSpec((n_fields, n_span, span, cells), lambda i: (0, i, 0, 0))
     field_shape = jax.ShapeDtypeStruct(fields.shape, F32)
     smooth, mixed = pl.pallas_call(
         span_kernel,
-        grid=(rows // 2,),
+        grid=(rows // n_span,),
         in_specs=[whole(), whole(), pair_block],
         out_specs=[pair_block, pair_block],
         out_shape=[pltpu.HBM(fields.shape, F32)] * 2,
@@ -535,7 +542,7 @@
         name="span",
     )(smooth_mat, mixed_mat, held_fields)
 
-    n_rate = 4
+    n_rate = 8
     rate_block = pl.BlockSpec((n_rate, span, cells), lambda i: (i, 0, 0))
     rate_shape = jax.ShapeDtypeStruct(rates_fwd.shape, F32)
     is_last = (section == sections - 1).astype(jnp.int32).reshape(1)
@@ -571,12 +578,12 @@
     end_fwd, end_bwd = gains[3], gains[4]
     gains = gains[:3]
     others = [
-        lax.ppermute(gains, "gx", [(at, (at + hop) % sections) for at in range(sections)])
+        lax.ppermute(gains, "gx", [(at, at ^ hop) for at in range(sections)])
         for hop in range(1, sections)
     ]
     arrivals = jnp.stack([gains] + others)
     every = jnp.stack([
-        lax.dynamic_index_in_dim(arrivals, (section - at) % sections, 0, False)
+        lax.dynamic_index_in_dim(arrivals, section ^ at, 0, False)
         for at in range(sections)
     ])
     gain_f, gain_b, gain_c = every[:, 0], every[:, 1], every[:, 2]
@@ -596,7 +603,7 @@
         start_gain.append(value)
         fwd_row, bwd_row = [], []
         for hop in range(1, sections):
-            source = (to - hop) % sections
+            source = to ^ hop
             value = one
             for at in range(min(source, to) + 1, max(source, to)):
                 value = value * (gain_f if source < to else gain_b)[at]
@@ -634,8 +641,8 @@
     upstream = first + turn_out[None] * last
     back = jnp.zeros_like(last)
     for hop in range(1, sections):
-        payload = jnp.where(section + hop < sections, last, upstream)
-        got = lax.ppermute(payload, "gx", [(at, (at + hop) % sections) for at in range(sections)])
+        payload = jnp.where((section ^ hop) > section, last, upstream)
+        got = lax.ppermute(payload, "gx", [(at, at ^ hop) for at in range(sections)])
         entering = entering + hop_fwd[hop - 1][None] * got
         back = back + hop_bwd[hop - 1][None] * got
     back = back + turn[None] * (own_gain[None] * entering + last)

time: 104 us -> 97.1 us (0.934)
  Pallas kernels: 73.3 us -> 68 us
  waiting for transfers between devices: 9.34 us -> 7.9 us
    pallas_call x2, Pallas kernels: 21.2 us -> 16.8 us  [the longest x1 12.1 us: shards(): pl.pallas_call(span_kernel, grid=(rows // n_span,), in_specs=[whole(), wh...]
    ppermute x6, waiting for transfers between devices: 7.12 us -> 5.68 us  [the longest x3 5.67 us: shards(): lax.ppermute(payload, 'gx', [(at, at ^ hop) for at in range(sections)])]
    pad x2 -> x0, local copies, waits for them, and re-layouts: 1.19 us -> none  [shards(): jnp.pad(mat, ((0, size - n_fields), (0, size - n_fields)))]
  transfers between devices with their start and end apart: 11 -> 11, of which waited for: 3 -> 3; matrix products, arithmetic and copies ran while one was open for 2% -> 1% of each run, Pallas kernels for 50% -> 49%
where the time goes in v2:
time: 97.1 us; the launch traced here: 96.2 us
  Pallas kernels  68 us (70%)
  starting transfers between devices  13.8 us (14%)
  waiting for transfers between devices  7.9 us (8%)
  local copies, waits for them, and re-layouts  5.23 us (5%)
  other arithmetic  0.99 us (1%)
    pallas_call x1, Pallas kernels, shards(): pl.pallas_call(functools.partial(sweep_kernel, rows), grid=(span // tile,...  23.6 us
    pallas_call x1, Pallas kernels, shards(): pl.pallas_call(span_kernel, grid=(rows // n_span,), in_specs=[whole(), wh...  12.1 us
    pallas_call x1, Pallas kernels, shards(): pl.pallas_call(close_kernel, grid=(rows // n_close,), in_specs=[gain_bloc...  10.2 us
    pallas_call x1, Pallas kernels, shards(): pl.pallas_call(taps_kernel, grid=(n_fields,), in_specs=[SMEM, pl.BlockSpe...  7.51 us
    pallas_call x1, Pallas kernels, shards(): pl.pallas_call(rates_kernel, grid=(rows // n_rate,), in_specs=[SMEM, whol...  6.26 us
    ppermute x3, waiting for transfers between devices, shards(): lax.ppermute(payload, 'gx', [(at, at ^ hop) for at in range(sections)])  5.67 us
    ppermute x3, starting transfers between devices, shards(): lax.ppermute(gains, 'gx', [(at, at ^ hop) for at in range(sections)])  4.77 us
    pallas_call x1, Pallas kernels, shards(): pl.pallas_call(mats_kernel, grid_spec=pltpu.PrefetchScalarGridSpec(num_sc...  4.71 us
  transfers between devices with their start and end apart: 11, of which 3 were waited for; matrix products, arithmetic and copies ran while one was open for 1% of the time, Pallas kernels for 49%

profile of v2, /device:TPU:0, one launch (start us, length us, event | category | flops | bytes accessed | tf_op | source)
XLA Modules:
  0.0 96.2 jit_solution(1033020086569290217)
XLA Ops:
  0.0 7.5 %taps.1 = (f32[6,5,48,128]{3,2,1,0:T(8,128)}, f32[6,5,48,128]{3,2,1,0:T(8,128)}) custom-call(f32[1536]{0:T(1024)} %constant.85.clone.taps_ref, f32[5,32,96,128]{3,2,1,0:T(8,128)} %x_ref.2), custom_call_target="tpu_custom_call" | custom-call | flops 23592960 | bytes 7864320 | tf_op jit(solution)/shard_map/taps/pallas_call | solution.py:501
  7.5 0.4 collective-permute-start
  7.9 0.4 dynamic_update_slice.10
  8.4 0.2 dynamic_update_slice.11.flux_wall_ref.flux_span_ref.visc_ref
  8.6 0.6 copy-done.15
  9.2 4.7 %mats.1 = (bf16[160,1152]{1,0:T(8,128)(2,1)}, bf16[480,1536]{1,0:T(8,128)(2,1)}) custom-call(s32[1]{0:T(128)} %bitcast.1.dev_ref, f32[24,8]{1,0:T(8,128)} %copy-done.15, f32[24,8]{1,0:T(8,128)} %copy-done.15, f32[24,8]{1,0:T(8,128)} %copy-done.15, bf16[160,24]{1,0:T(8,128)(2,1)} %constant.90.clone.wall_rows_ref, f32[8,384]{1,0:T(8,128)} %constant.91.clone.wall_cols_ref, ...), custom_call_target="tpu_custom_call" | custom-call | flops 10000000 | bytes 8000000 | tf_op jit(solution)/shard_map/mats/pallas_call | solution.py:460
  13.9 1.1 %copy-done.1 = f32[6,5,48,128]{3,2,1,0:T(8,128)S(1)} copy-done((f32[6,5,48,128]{3,2,1,0:T(8,128)S(1)}, f32[6,5,48,128]{3,2,1,0:T(8,128)}, u32[]{:S(2)}) %copy-start.1) | copy-done | bytes 737304
  15.0 1.6 %chip.1 = (f32[3,240,128]{2,1,0:T(8,128)S(1)}, f32[3,240,128]{2,1,0:T(8,128)S(1)}, f32[3,240,128]{2,1,0:T(8,128)S(1)}) custom-call(f32[288]{0:T(512)S(1)} %copy-done.5, f32[6,240,128]{2,1,0:T(8,128)S(1)} %bitcast.82, f32[6,240,128]{2,1,0:T(8,128)} %collective-permute-done.other_ref), custom_call_target="tpu_custom_call" | custom-call | flops 1105920 | bytes 2211840 | tf_op jit(solution)/shard_map/chip/pallas_call | solution.py:516
  16.6 0.0 copy-start.7
  16.6 2.6 %collective-permute-start.1 = (f32[3,240,128]{2,1,0:T(8,128)S(1)}, f32[3,240,128]{2,1,0:T(8,128)S(1)}, u32[]{:S(2)}, u32[]{:S(2)}) collective-permute-start(f32[3,240,128]{2,1,0:T(8,128)S(1)} %get-tuple-element.58), channel_id=1, source_target_pairs={{0,2},{1,3},{2,0},{3,1},{4,6},{5,7},{6,4},{7,5},{8,10},{9,11},{10,... | collective-permute-start | bytes 1105928 | tf_op jit(solution)/shard_map/ppermute | solution.py:528
  19.2 1.5 %collective-permute-start.2 = (f32[3,240,128]{2,1,0:T(8,128)S(1)}, f32[3,240,128]{2,1,0:T(8,128)S(1)}, u32[]{:S(2)}, u32[]{:S(2)}) collective-permute-start(f32[3,240,128]{2,1,0:T(8,128)S(1)} %get-tuple-element.59), channel_id=1, source_target_pairs={{0,4},{1,5},{2,6},{3,7},{4,0},{5,1},{6,2},{7,3},{8,12},{9,13},{10,... | collective-permute-start | bytes 1105928 | tf_op jit(solution)/shard_map/ppermute | solution.py:528
  20.8 0.0 collective-permute-start.3
  20.8 1.4 %copy-done.8 = bf16[480,1536]{1,0:T(8,128)(2,1)S(1)} copy-done((bf16[480,1536]{1,0:T(8,128)(2,1)S(1)}, bf16[480,1536]{1,0:T(8,128)(2,1)}, u32[]{:S(2)}) %copy-start.8) | copy-done | bytes 1474584
  22.2 12.1 %span.1 = (f32[5,32,96,128]{3,2,1,0:T(8,128)}, f32[5,32,96,128]{3,2,1,0:T(8,128)}) custom-call(bf16[96,288]{1,0:T(8,128)(2,1)S(1)} %copy-done.11, bf16[480,1536]{1,0:T(8,128)(2,1)S(1)} %copy-done.8, f32[5,32,96,128]{3,2,1,0:T(8,128)S(1)} %copy-done), custom_call_target="tpu_custom_call" | custom-call | flops 15728640000 | bytes 23592960 | tf_op jit(solution)/shard_map/span/pallas_call | solution.py:534
  34.3 0.0 copy-start.3
  34.3 0.0 copy-start.4
  34.3 6.3 %rates.1 = (f32[32,96,128]{2,1,0:T(8,128)}, f32[32,96,128]{2,1,0:T(8,128)}, f32[32,96,128]{2,1,0:T(8,128)}, f32[32,96,128]{2,1,0:T(8,128)}, f32[32,96,128]{2,1,0...) custom-call(s32[1]{0:T(128)} %bitcast.last_ref, bf16[2,384,256]{2,1,0:T(8,128)(2,1)S(1)} %copy-done.10, ...), custom_call_target="tpu_custom_call" | custom-call | flops 3145728000 | bytes 12582912 | tf_op jit(solution)/shard_map/rates/pallas_call | solution.py:555
  40.6 2.0 %states.1 = (f32[6,240,128]{2,1,0:T(8,128)S(1)}, f32[6,240,128]{2,1,0:T(8,128)S(1)}) custom-call(f32[432]{0:T(512)S(1)} %copy-done.3, f32[288]{0:T(512)S(1)} %copy-done.4, f32[6,240,128]{2,1,0:T(8,128)S(1)} %bitcast.83, f32[6,240,128]{2,1,0:T(8,128)} %collective-permute-done.other_ref, f32[3,240,128]{2,1,0:T(8,128)S(1)} %collective-permute-done.1.refs_0_, ...), custom_call_target="tpu_custom_call" | custom-call | flops 3686400 | bytes 3686400 | tf_op jit(solution)/shard_map/states/pallas_call | solution.py:567
  42.7 0.9 copy-done.9
  43.6 2.2 %collective-permute-done.4 = f32[6,240,128]{2,1,0:T(8,128)S(1)} collective-permute-done((f32[6,240,128]{2,1,0:T(8,128)S(1)}, f32[6,240,128]{2,1,0:T(8,128)S(1)}, u32[]{:S(2)}, u32[]{:S(2)}) %collective-permute-start.4) | collective-permute-done | bytes 737312 | tf_op jit(solution)/shard_map/ppermute | solution.py:576
  45.8 4.1 %collective-permute-start.7 = (f32[3,32,128]{2,1,0:T(8,128)S(1)}, f32[3,32,128]{2,1,0:T(8,128)S(1)}, u32[]{:S(2)}, u32[]{:S(2)}) collective-permute-start(f32[3,32,128]{2,1,0:T(8,128)S(1)} %get-tuple-element.109), channel_id=1, source_target_pairs={{0,24},{8,16},{16,8},{24,0},{1,25},{9,17},{17,9},{25,1},{2,26},{10... | collective-permute-start | bytes 147464 | tf_op jit(solution)/shard_map/ppermute | solution.py:581
  49.9 0.6 collective-permute-start.5
  50.6 23.6 %sweep.1 = (f32[160,96,128]{2,1,0:T(8,128)}, f32[160,128]{1,0:T(8,128)}, f32[160,128]{1,0:T(8,128)}) custom-call(bf16[96,288]{1,0:T(8,128)(2,1)} %constant.89.clone.smooth_ref, bf16[480,1536]{1,0:T(8,128)(2,1)} %get-tuple-element.53.mixed_ref, bf16[160,1152]{1,0:T(8,128)(2,1)} %get-tuple-element.67.wall_ref, bf16[2,256,256]{2,1,0:T(8,128)(2,1)} %constant.104.sums_ref, ...), custom_call_target="tpu_custom_call" | custom-call | flops 11796480000 | bytes 23592960 | tf_op jit(solution)/shard_map/sweep/pallas_call | solution.py:625
  74.4 0.1 fusion.11
  74.6 0.5 copy-done.14
  75.1 0.0 copy-done.16
  75.1 3.8 %collective-permute-start.10 = (f32[5,32,128]{2,1,0:T(8,128)S(1)}, f32[5,32,128]{2,1,0:T(8,128)S(1)}, u32[]{:S(2)}, u32[]{:S(2)}) collective-permute-start(f32[5,32,128]{2,1,0:T(8,128)S(1)} %get-tuple-element.95), channel_id=1, source_target_pairs={{0,24},{8,16},{16,8},{24,0},{1,25},{9,17},{17,9},{25,1},{2,26},{10... | collective-permute-start | bytes 245768 | tf_op jit(solution)/shard_map/ppermute | solution.py:645
  78.9 0.7 collective-permute-start.8
  79.6 2.6 %collective-permute-done.10 = f32[5,32,128]{2,1,0:T(8,128)S(1)} collective-permute-done((f32[5,32,128]{2,1,0:T(8,128)S(1)}, f32[5,32,128]{2,1,0:T(8,128)S(1)}, u32[]{:S(2)}, u32[]{:S(2)}) %collective-permute-start.10) | collective-permute-done | bytes 81952 | tf_op jit(solution)/shard_map/ppermute | solution.py:645
  82.2 3.1 %collective-permute-done.9 = f32[5,32,128]{2,1,0:T(8,128)S(1)} collective-permute-done((f32[5,32,128]{2,1,0:T(8,128)S(1)}, f32[5,32,128]{2,1,0:T(8,128)S(1)}, u32[]{:S(2)}, u32[]{:S(2)}) %collective-permute-start.9) | collective-permute-done | bytes 81952 | tf_op jit(solution)/shard_map/ppermute | solution.py:645
  85.3 0.7 multiply_add_fusion
  86.0 10.2 %close.1 = f32[5,32,96,128]{3,2,1,0:T(8,128)} custom-call(f32[32,96,128]{2,1,0:T(8,128)} %get-tuple-element.51.carry_ref, f32[32,96,128]{2,1,0:T(8,128)} %get-tuple-element.52.tail_ref, f32[5,32,128]{2,1,0:T(8,128)} %get-tuple-element.80.enter_ref, f32[5,32,128]{2,1,0:T(8,128)} %get-tuple-element.79.back_ref, f32[5,32,96,128]{3,2,1,0:T(8,128)} %bitcast.87), custom_call_target="tpu_custom_call" | custom-call | flops 7864320 | bytes 19660800 | tf_op jit(solution)/shard_map/close/pallas_call | solution.py:654
  (64 shorter events, 0.3 us)
Async XLA Ops:
  0.0 7.9 %copy-start.20 = (f32[5,5]{1,0:T(8,128)S(1)}, f32[5,5]{1,0:T(8,128)}, u32[]{:S(2)}) copy-start(f32[5,5]{1,0:T(8,128)} %param.25) | copy-start | bytes 304
  0.0 7.9 %copy-start.19 = (f32[5,5]{1,0:T(8,128)S(1)}, f32[5,5]{1,0:T(8,128)}, u32[]{:S(2)}) copy-start(f32[5,5]{1,0:T(8,128)} %param.26) | copy-start | bytes 304
  0.0 8.4 %copy-start.21 = (f32[5]{0:T(128)S(1)}, f32[5]{0:T(128)}, u32[]{:S(2)}) copy-start(f32[5]{0:T(128)} %param.27) | copy-start | bytes 64
  7.5 6.4 %collective-permute-start = (f32[6,240,128]{2,1,0:T(8,128)}, f32[6,240,128]{2,1,0:T(8,128)}, u32[]{:S(2)}, u32[]{:S(2)}) collective-permute-start(f32[6,240,128]{2,1,0:T(8,128)} %bitcast.97), channel_id=1, source_target_pairs={{0,1},{1,0},{2,3},{3,2},{4,5},{5,4},{6,7},{7,6},{8,9},{9,8},{10,11... | collective-permute-start | bytes 2211848 | tf_op jit(solution)/shard_map/ppermute | solution.py:514
  9.2 4.7 %copy-start.5 = (f32[288]{0:T(512)S(1)}, f32[288]{0:T(512)}, u32[]{:S(2)}) copy-start(f32[288]{0:T(512)} %constant.86.clone.mix_ref) | copy-start | bytes 3460
  9.2 11.6 %copy-start = (f32[5,32,96,128]{3,2,1,0:T(8,128)S(1)}, f32[5,32,96,128]{3,2,1,0:T(8,128)}, u32[]{:S(2)}) copy-start(f32[5,32,96,128]{3,2,1,0:T(8,128)} %x_ref.2) | copy-start | bytes 23592964
  9.2 11.6 %copy-start.11 = (bf16[96,288]{1,0:T(8,128)(2,1)S(1)}, bf16[96,288]{1,0:T(8,128)(2,1)}, u32[]{:S(2)}) copy-start(bf16[96,288]{1,0:T(8,128)(2,1)} %constant.89.clone.smooth_ref) | copy-start | bytes 165892
  13.9 1.1 %copy-start.1 = (f32[6,5,48,128]{3,2,1,0:T(8,128)S(1)}, f32[6,5,48,128]{3,2,1,0:T(8,128)}, u32[]{:S(2)}) copy-start(f32[6,5,48,128]{3,2,1,0:T(8,128)} %get-tuple-element.44) | copy-start | bytes 2211844
  16.6 17.7 %copy-start.6 = (f32[32,96,128]{2,1,0:T(8,128)S(1)}, f32[32,96,128]{2,1,0:T(8,128)}, u32[]{:S(2)}) copy-start(f32[32,96,128]{2,1,0:T(8,128)} %fwd_ref) | copy-start | bytes 4718596
  16.6 17.7 %copy-start.7 = (f32[32,96,128]{2,1,0:T(8,128)S(1)}, f32[32,96,128]{2,1,0:T(8,128)}, u32[]{:S(2)}) copy-start(f32[32,96,128]{2,1,0:T(8,128)} %bwd_ref) | copy-start | bytes 4718596
  16.6 24.0 %collective-permute-start.1 = (f32[3,240,128]{2,1,0:T(8,128)S(1)}, f32[3,240,128]{2,1,0:T(8,128)S(1)}, u32[]{:S(2)}, u32[]{:S(2)}) collective-permute-start(f32[3,240,128]{2,1,0:T(8,128)S(1)} %get-tuple-element.58), channel_id=1, source_target_pairs={{0,2},{1,3},{2,0},{3,1},{4,6},{5,7},{6,4},{7,5},{8,10},{9,11},{10,... | collective-permute-start | bytes 1105928 | tf_op jit(solution)/shard_map/ppermute | solution.py:528
  19.2 21.4 %collective-permute-start.2 = (f32[3,240,128]{2,1,0:T(8,128)S(1)}, f32[3,240,128]{2,1,0:T(8,128)S(1)}, u32[]{:S(2)}, u32[]{:S(2)}) collective-permute-start(f32[3,240,128]{2,1,0:T(8,128)S(1)} %get-tuple-element.59), channel_id=1, source_target_pairs={{0,4},{1,5},{2,6},{3,7},{4,0},{5,1},{6,2},{7,3},{8,12},{9,13},{10,... | collective-permute-start | bytes 1105928 | tf_op jit(solution)/shard_map/ppermute | solution.py:528
  20.8 19.9 %collective-permute-start.3 = (f32[3,240,128]{2,1,0:T(8,128)S(1)}, f32[3,240,128]{2,1,0:T(8,128)S(1)}, u32[]{:S(2)}, u32[]{:S(2)}) collective-permute-start(f32[3,240,128]{2,1,0:T(8,128)S(1)} %get-tuple-element.60), channel_id=1, source_target_pairs={{0,6},{1,7},{2,4},{3,5},{4,2},{5,3},{6,0},{7,1},{8,14},{9,15},{10,... | collective-permute-start | bytes 1105928 | tf_op jit(solution)/shard_map/ppermute | solution.py:528
  20.8 1.4 %copy-start.8 = (bf16[480,1536]{1,0:T(8,128)(2,1)S(1)}, bf16[480,1536]{1,0:T(8,128)(2,1)}, u32[]{:S(2)}) copy-start(bf16[480,1536]{1,0:T(8,128)(2,1)} %get-tuple-element.53.mixed_ref) | copy-start | bytes 4423684
  22.1 12.1 %copy-start.10 = (bf16[2,384,256]{2,1,0:T(8,128)(2,1)S(1)}, bf16[2,384,256]{2,1,0:T(8,128)(2,1)}, u32[]{:S(2)}) copy-start(bf16[2,384,256]{2,1,0:T(8,128)(2,1)} %constant.103.logs_ref) | copy-start | bytes 1179652
  22.1 12.1 %copy-start.12 = (bf16[256,128]{1,0:T(8,128)(2,1)S(1)}, bf16[256,128]{1,0:T(8,128)(2,1)}, u32[]{:S(2)}) copy-start(bf16[256,128]{1,0:T(8,128)(2,1)} %constant.106.sums_ref) | copy-start | bytes 196612
  22.2 12.1 %copy-start.13 = (bf16[3,16,384]{2,1,0:T(8,128)(2,1)S(1)}, bf16[3,16,384]{2,1,0:T(8,128)(2,1)}, u32[]{:S(2)}) copy-start(bf16[3,16,384]{2,1,0:T(8,128)(2,1)} %constant.98.clone.ends_ref) | copy-start | bytes 110596
  34.3 6.3 %copy-start.2 = (f32[6,5,48,128]{3,2,1,0:T(8,128)S(1)}, f32[6,5,48,128]{3,2,1,0:T(8,128)}, u32[]{:S(2)}) copy-start(f32[6,5,48,128]{3,2,1,0:T(8,128)} %get-tuple-element.44) | copy-start | bytes 2211844
  34.3 6.3 %copy-start.3 = (f32[432]{0:T(512)S(1)}, f32[432]{0:T(512)}, u32[]{:S(2)}) copy-start(f32[432]{0:T(512)} %constant.87.clone.from_ref) | copy-start | bytes 5188
  34.3 6.3 %copy-start.4 = (f32[288]{0:T(512)S(1)}, f32[288]{0:T(512)}, u32[]{:S(2)}) copy-start(f32[288]{0:T(512)} %constant.88.clone.to_ref) | copy-start | bytes 3460
  43.6 2.2 %collective-permute-start.4 = (f32[6,240,128]{2,1,0:T(8,128)S(1)}, f32[6,240,128]{2,1,0:T(8,128)S(1)}, u32[]{:S(2)}, u32[]{:S(2)}) collective-permute-start(f32[6,240,128]{2,1,0:T(8,128)S(1)} %get-tuple-element.64), channel_id=1, source_target_pairs={{0,1},{1,0},{2,3},{3,2},{4,5},{5,4},{6,7},{7,6},{8,9},{9,8},{10,11... | collective-permute-start | bytes 2211848 | tf_op jit(solution)/shard_map/ppermute | solution.py:576
  45.8 4.8 %copy-start.22 = (f32[6,240,128]{2,1,0:T(8,128)}, f32[6,240,128]{2,1,0:T(8,128)S(1)}, u32[]{:S(2)}) copy-start(f32[6,240,128]{2,1,0:T(8,128)S(1)} %collective-permute-done.4) | copy-start | bytes 2211844
  45.8 28.4 %collective-permute-start.7 = (f32[3,32,128]{2,1,0:T(8,128)S(1)}, f32[3,32,128]{2,1,0:T(8,128)S(1)}, u32[]{:S(2)}, u32[]{:S(2)}) collective-permute-start(f32[3,32,128]{2,1,0:T(8,128)S(1)} %get-tuple-element.109), channel_id=1, source_target_pairs={{0,24},{8,16},{16,8},{24,0},{1,25},{9,17},{17,9},{25,1},{2,26},{10... | collective-permute-start | bytes 147464 | tf_op jit(solution)/shard_map/ppermute | solution.py:581
  49.9 24.3 %collective-permute-start.6 = (f32[3,32,128]{2,1,0:T(8,128)S(1)}, f32[3,32,128]{2,1,0:T(8,128)S(1)}, u32[]{:S(2)}, u32[]{:S(2)}) collective-permute-start(f32[3,32,128]{2,1,0:T(8,128)S(1)} %get-tuple-element.109), channel_id=1, source_target_pairs={{0,16},{8,24},{16,0},{24,8},{1,17},{9,25},{17,1},{25,9},{2,18},{10... | collective-permute-start | bytes 147464 | tf_op jit(solution)/shard_map/ppermute | solution.py:581
  49.9 24.3 %collective-permute-start.5 = (f32[3,32,128]{2,1,0:T(8,128)S(1)}, f32[3,32,128]{2,1,0:T(8,128)S(1)}, u32[]{:S(2)}, u32[]{:S(2)}) collective-permute-start(f32[3,32,128]{2,1,0:T(8,128)S(1)} %get-tuple-element.109), channel_id=1, source_target_pairs={{0,8},{8,0},{16,24},{24,16},{1,9},{9,1},{17,25},{25,17},{2,10},{10... | collective-permute-start | bytes 147464 | tf_op jit(solution)/shard_map/ppermute | solution.py:581
  50.6 23.8 %copy-start.18 = (f32[1,3,32,128]{3,2,1,0:T(8,128)S(1)}, f32[1,3,32,128]{3,2,1,0:T(8,128)}, u32[]{:S(2)}) copy-start(f32[1,3,32,128]{3,2,1,0:T(8,128)} %constant.84.clone.1) | copy-start | bytes 147460
  74.2 0.9 copy-start.14
  74.2 0.9 copy-start.16
  74.3 11.1 %copy-start.17 = (f32[5,32,96]{2,1,0:T(8,128)S(1)}, f32[5,32,96]{2,1,0:T(8,128)}, u32[]{:S(2)}) copy-start(f32[5,32,96]{2,1,0:T(8,128)} %param.22) | copy-start | bytes 184324
  75.1 7.0 %collective-permute-start.10 = (f32[5,32,128]{2,1,0:T(8,128)S(1)}, f32[5,32,128]{2,1,0:T(8,128)S(1)}, u32[]{:S(2)}, u32[]{:S(2)}) collective-permute-start(f32[5,32,128]{2,1,0:T(8,128)S(1)} %get-tuple-element.95), channel_id=1, source_target_pairs={{0,24},{8,16},{16,8},{24,0},{1,25},{9,17},{17,9},{25,1},{2,26},{10... | collective-permute-start | bytes 245768 | tf_op jit(solution)/shard_map/ppermute | solution.py:645
  78.9 6.4 %collective-permute-start.9 = (f32[5,32,128]{2,1,0:T(8,128)S(1)}, f32[5,32,128]{2,1,0:T(8,128)S(1)}, u32[]{:S(2)}, u32[]{:S(2)}) collective-permute-start(f32[5,32,128]{2,1,0:T(8,128)S(1)} %get-tuple-element.96), channel_id=1, source_target_pairs={{0,16},{8,24},{16,0},{24,8},{1,17},{9,25},{17,1},{25,9},{2,18},{10... | collective-permute-start | bytes 245768 | tf_op jit(solution)/shard_map/ppermute | solution.py:645
  78.9 6.4 %collective-permute-start.8 = (f32[5,32,128]{2,1,0:T(8,128)S(1)}, f32[5,32,128]{2,1,0:T(8,128)S(1)}, u32[]{:S(2)}, u32[]{:S(2)}) collective-permute-start(f32[5,32,128]{2,1,0:T(8,128)S(1)} %get-tuple-element.94), channel_id=1, source_target_pairs={{0,8},{8,0},{16,24},{24,16},{1,9},{9,1},{17,25},{25,17},{2,10},{10... | collective-permute-start | bytes 245768 | tf_op jit(solution)/shard_map/ppermute | solution.py:645
  (2 other events, 1.5 us)

commit v3 on v2

--- a/solution.py
+++ b/solution.py
@@ -10,7 +10,7 @@
 
 F32, BF16 = jnp.float32, jnp.bfloat16
 STEP = 0.5
-LIMITS = {"mats": 56, "taps": 56, "chip": 8, "span": 24, "rates": 24, "states": 10, "sweep": 56, "close": 56}
+LIMITS = {"mats": 56, "taps": 56, "chip": 8, "span": 24, "rates": 24, "states": 10, "sweep": 52, "close": 16}
 
 
 def tridiagonal(points, below, centre, above, periodic):
@@ -627,7 +627,7 @@
         grid=(span // tile,),
         in_specs=[whole()] * 6 + [line_block] * 2 + [rate_tile] * 4,
         out_specs=[line_block, end_block, end_block],
-        out_shape=[jax.ShapeDtypeStruct((lines, span, cells), F32), end_shape, end_shape],
+        out_shape=[pltpu.VMEM((lines, span, cells), F32), end_shape, end_shape],
         scratch_shapes=[
             pltpu.VMEM((n_us * span, cells), F32), pltpu.VMEM((n_ws * span, cells), F32)],
         compiler_params=params(LIMITS["sweep"]),

time: 97.1 us -> 92.6 us (0.954)
  Pallas kernels: 68 us -> 64.6 us
    pallas_call x1, Pallas kernels: 10.2 us -> 7.23 us  [shards(): pl.pallas_call(close_kernel, grid=(rows // n_close,), in_specs=[gain_bloc...]
    unnamed x46 -> x50, local copies, waits for them, and re-layouts: 4.56 us -> 4.55 us
  transfers between devices with their start and end apart: 11 -> 11, of which waited for: 3 -> 3; matrix products, arithmetic and copies ran while one was open for 1% -> 1% of each run, Pallas kernels for 49% -> 50%
where the time goes in v3:
time: 92.6 us; the launch traced here: 92.3 us
  Pallas kernels  64.6 us (70%)
  starting transfers between devices  13.8 us (15%)
  waiting for transfers between devices  7.91 us (9%)
  local copies, waits for them, and re-layouts  5.21 us (6%)
    pallas_call x1, Pallas kernels, shards(): pl.pallas_call(functools.partial(sweep_kernel, rows), grid=(span // tile,...  23.3 us
    pallas_call x1, Pallas kernels, shards(): pl.pallas_call(span_kernel, grid=(rows // n_span,), in_specs=[whole(), wh...  12.1 us
    pallas_call x1, Pallas kernels, shards(): pl.pallas_call(taps_kernel, grid=(n_fields,), in_specs=[SMEM, pl.BlockSpe...  7.51 us
    pallas_call x1, Pallas kernels, shards(): pl.pallas_call(close_kernel, grid=(rows // n_close,), in_specs=[gain_bloc...  7.23 us
    pallas_call x1, Pallas kernels, shards(): pl.pallas_call(rates_kernel, grid=(rows // n_rate,), in_specs=[SMEM, whol...  6.21 us
    ppermute x3, waiting for transfers between devices, shards(): lax.ppermute(payload, 'gx', [(at, at ^ hop) for at in range(sections)])  5.68 us
    ppermute x3, starting transfers between devices, shards(): lax.ppermute(gains, 'gx', [(at, at ^ hop) for at in range(sections)])  4.77 us
    pallas_call x1, Pallas kernels, shards(): pl.pallas_call(mats_kernel, grid_spec=pltpu.PrefetchScalarGridSpec(num_sc...  4.71 us
  transfers between devices with their start and end apart: 11, of which 3 were waited for; matrix products, arithmetic and copies ran while one was open for 1% of the time, Pallas kernels for 50%

profile of v3, /device:TPU:0, one launch (start us, length us, event | category | flops | bytes accessed | tf_op | source)
XLA Modules:
  0.0 92.3 jit_solution(4745668684119275429)
XLA Ops:
  0.0 7.5 %taps.1 = (f32[6,5,48,128]{3,2,1,0:T(8,128)}, f32[6,5,48,128]{3,2,1,0:T(8,128)}) custom-call(f32[1536]{0:T(1024)} %constant.85.clone.taps_ref, f32[5,32,96,128]{3,2,1,0:T(8,128)} %x_ref.2), custom_call_target="tpu_custom_call" | custom-call | flops 23592960 | bytes 7864320 | tf_op jit(solution)/shard_map/taps/pallas_call | solution.py:501
  7.5 0.4 collective-permute-start
  7.9 0.4 dynamic_update_slice.10
  8.4 0.2 dynamic_update_slice.11.flux_wall_ref.flux_span_ref.visc_ref
  8.6 0.6 copy-done.17
  9.2 4.7 %mats.1 = (bf16[160,1152]{1,0:T(8,128)(2,1)}, bf16[480,1536]{1,0:T(8,128)(2,1)}) custom-call(s32[1]{0:T(128)} %bitcast.1.dev_ref, f32[24,8]{1,0:T(8,128)} %copy-done.17, f32[24,8]{1,0:T(8,128)} %copy-done.17, f32[24,8]{1,0:T(8,128)} %copy-done.17, bf16[160,24]{1,0:T(8,128)(2,1)} %constant.90.clone.wall_rows_ref, f32[8,384]{1,0:T(8,128)} %constant.91.clone.wall_cols_ref, ...), custom_call_target="tpu_custom_call" | custom-call | flops 10000000 | bytes 8000000 | tf_op jit(solution)/shard_map/mats/pallas_call | solution.py:460
  13.9 1.1 %copy-done.1 = f32[6,5,48,128]{3,2,1,0:T(8,128)S(1)} copy-done((f32[6,5,48,128]{3,2,1,0:T(8,128)S(1)}, f32[6,5,48,128]{3,2,1,0:T(8,128)}, u32[]{:S(2)}) %copy-start.1) | copy-done | bytes 737304
  15.0 1.6 %chip.1 = (f32[3,240,128]{2,1,0:T(8,128)S(1)}, f32[3,240,128]{2,1,0:T(8,128)S(1)}, f32[3,240,128]{2,1,0:T(8,128)S(1)}) custom-call(f32[288]{0:T(512)S(1)} %copy-done.7, f32[6,240,128]{2,1,0:T(8,128)S(1)} %bitcast.83, f32[6,240,128]{2,1,0:T(8,128)} %collective-permute-done.other_ref), custom_call_target="tpu_custom_call" | custom-call | flops 1105920 | bytes 2211840 | tf_op jit(solution)/shard_map/chip/pallas_call | solution.py:516
  16.6 0.0 copy-start.8
  16.6 2.6 %collective-permute-start.1 = (f32[3,240,128]{2,1,0:T(8,128)S(1)}, f32[3,240,128]{2,1,0:T(8,128)S(1)}, u32[]{:S(2)}, u32[]{:S(2)}) collective-permute-start(f32[3,240,128]{2,1,0:T(8,128)S(1)} %get-tuple-element.58), channel_id=1, source_target_pairs={{0,2},{1,3},{2,0},{3,1},{4,6},{5,7},{6,4},{7,5},{8,10},{9,11},{10,... | collective-permute-start | bytes 1105928 | tf_op jit(solution)/shard_map/ppermute | solution.py:528
  19.2 1.5 %collective-permute-start.2 = (f32[3,240,128]{2,1,0:T(8,128)S(1)}, f32[3,240,128]{2,1,0:T(8,128)S(1)}, u32[]{:S(2)}, u32[]{:S(2)}) collective-permute-start(f32[3,240,128]{2,1,0:T(8,128)S(1)} %get-tuple-element.59), channel_id=1, source_target_pairs={{0,4},{1,5},{2,6},{3,7},{4,0},{5,1},{6,2},{7,3},{8,12},{9,13},{10,... | collective-permute-start | bytes 1105928 | tf_op jit(solution)/shard_map/ppermute | solution.py:528
  20.8 0.0 collective-permute-start.3
  20.8 1.4 %copy-done.10 = bf16[480,1536]{1,0:T(8,128)(2,1)S(1)} copy-done((bf16[480,1536]{1,0:T(8,128)(2,1)S(1)}, bf16[480,1536]{1,0:T(8,128)(2,1)}, u32[]{:S(2)}) %copy-start.10) | copy-done | bytes 1474584
  22.2 12.1 %span.1 = (f32[5,32,96,128]{3,2,1,0:T(8,128)}, f32[5,32,96,128]{3,2,1,0:T(8,128)}) custom-call(bf16[96,288]{1,0:T(8,128)(2,1)S(1)} %copy-done.13, bf16[480,1536]{1,0:T(8,128)(2,1)S(1)} %copy-done.10, f32[5,32,96,128]{3,2,1,0:T(8,128)S(1)} %copy-done), custom_call_target="tpu_custom_call" | custom-call | flops 15728640000 | bytes 23592960 | tf_op jit(solution)/shard_map/span/pallas_call | solution.py:534
  34.3 0.0 copy-start.5
  34.3 0.0 copy-start.6
  34.4 6.2 %rates.1 = (f32[32,96,128]{2,1,0:T(8,128)}, f32[32,96,128]{2,1,0:T(8,128)}, f32[32,96,128]{2,1,0:T(8,128)}, f32[32,96,128]{2,1,0:T(8,128)}, f32[32,96,128]{2,1,0...) custom-call(s32[1]{0:T(128)} %bitcast.last_ref, bf16[2,384,256]{2,1,0:T(8,128)(2,1)S(1)} %copy-done.12, ...), custom_call_target="tpu_custom_call" | custom-call | flops 3145728000 | bytes 12582912 | tf_op jit(solution)/shard_map/rates/pallas_call | solution.py:555
  40.6 2.0 %states.1 = (f32[6,240,128]{2,1,0:T(8,128)S(1)}, f32[6,240,128]{2,1,0:T(8,128)S(1)}) custom-call(f32[432]{0:T(512)S(1)} %copy-done.5, f32[288]{0:T(512)S(1)} %copy-done.6, f32[6,240,128]{2,1,0:T(8,128)S(1)} %bitcast.84, f32[6,240,128]{2,1,0:T(8,128)} %collective-permute-done.other_ref, f32[3,240,128]{2,1,0:T(8,128)S(1)} %collective-permute-done.1.refs_0_, ...), custom_call_target="tpu_custom_call" | custom-call | flops 3686400 | bytes 3686400 | tf_op jit(solution)/shard_map/states/pallas_call | solution.py:567
  42.7 0.9 copy-done.11
  43.5 2.2 %collective-permute-done.4 = f32[6,240,128]{2,1,0:T(8,128)S(1)} collective-permute-done((f32[6,240,128]{2,1,0:T(8,128)S(1)}, f32[6,240,128]{2,1,0:T(8,128)S(1)}, u32[]{:S(2)}, u32[]{:S(2)}) %collective-permute-start.4) | collective-permute-done | bytes 737312 | tf_op jit(solution)/shard_map/ppermute | solution.py:576
  45.7 4.1 %collective-permute-start.7 = (f32[3,32,128]{2,1,0:T(8,128)S(1)}, f32[3,32,128]{2,1,0:T(8,128)S(1)}, u32[]{:S(2)}, u32[]{:S(2)}) collective-permute-start(f32[3,32,128]{2,1,0:T(8,128)S(1)} %get-tuple-element.109), channel_id=1, source_target_pairs={{0,24},{8,16},{16,8},{24,0},{1,25},{9,17},{17,9},{25,1},{2,26},{10... | collective-permute-start | bytes 147464 | tf_op jit(solution)/shard_map/ppermute | solution.py:581
  49.9 0.6 collective-permute-start.5
  50.5 23.3 %sweep.1 = (f32[160,96,128]{2,1,0:T(8,128)S(1)}, f32[160,128]{1,0:T(8,128)}, f32[160,128]{1,0:T(8,128)}) custom-call(bf16[96,288]{1,0:T(8,128)(2,1)} %constant.89.clone.smooth_ref, bf16[480,1536]{1,0:T(8,128)(2,1)} %get-tuple-element.53.mixed_ref, bf16[160,1152]{1,0:T(8,128)(2,1)} %get-tuple-element.67.wall_ref, bf16[2,256,256]{2,1,0:T(8,128)(2,1)} %constant.104.sums_ref, ...), custom_call_target="tpu_custom_call" | custom-call | flops 11796480000 | bytes 23592960 | tf_op jit(solution)/shard_map/sweep/pallas_call | solution.py:625
  74.1 0.1 fusion.11
  74.2 0.5 copy-done.16
  74.7 0.0 copy-done.18
  74.8 3.8 %collective-permute-start.10 = (f32[5,32,128]{2,1,0:T(8,128)S(1)}, f32[5,32,128]{2,1,0:T(8,128)S(1)}, u32[]{:S(2)}, u32[]{:S(2)}) collective-permute-start(f32[5,32,128]{2,1,0:T(8,128)S(1)} %get-tuple-element.95), channel_id=1, source_target_pairs={{0,24},{8,16},{16,8},{24,0},{1,25},{9,17},{17,9},{25,1},{2,26},{10... | collective-permute-start | bytes 245768 | tf_op jit(solution)/shard_map/ppermute | solution.py:645
  78.6 0.6 collective-permute-start.8
  79.3 2.6 %collective-permute-done.10 = f32[5,32,128]{2,1,0:T(8,128)S(1)} collective-permute-done((f32[5,32,128]{2,1,0:T(8,128)S(1)}, f32[5,32,128]{2,1,0:T(8,128)S(1)}, u32[]{:S(2)}, u32[]{:S(2)}) %collective-permute-start.10) | collective-permute-done | bytes 81952 | tf_op jit(solution)/shard_map/ppermute | solution.py:645
  81.8 3.1 %collective-permute-done.9 = f32[5,32,128]{2,1,0:T(8,128)S(1)} collective-permute-done((f32[5,32,128]{2,1,0:T(8,128)S(1)}, f32[5,32,128]{2,1,0:T(8,128)S(1)}, u32[]{:S(2)}, u32[]{:S(2)}) %collective-permute-start.9) | collective-permute-done | bytes 81952 | tf_op jit(solution)/shard_map/ppermute | solution.py:645
  84.9 0.1 multiply_add_fusion
  85.0 7.2 %close.1 = f32[5,32,96,128]{3,2,1,0:T(8,128)} custom-call(f32[32,96,128]{2,1,0:T(8,128)S(1)} %copy-done.3, f32[32,96,128]{2,1,0:T(8,128)S(1)} %copy-done.4, f32[5,32,128]{2,1,0:T(8,128)S(1)} %get-tuple-element.80.enter_ref, f32[5,32,128]{2,1,0:T(8,128)S(1)} %get-tuple-element.79.back_ref, f32[5,32,96,128]{3,2,1,0:T(8,128)S(1)} %bitcast.82), custom_call_target="tpu_custom_call" | custom-call | flops 7864320 | bytes 19660800 | tf_op jit(solution)/shard_map/close/pallas_call | solution.py:654
  (68 shorter events, 0.3 us)
Async XLA Ops:
  0.0 7.9 %copy-start.22 = (f32[5,5]{1,0:T(8,128)S(1)}, f32[5,5]{1,0:T(8,128)}, u32[]{:S(2)}) copy-start(f32[5,5]{1,0:T(8,128)} %param.25) | copy-start | bytes 304
  0.0 7.9 %copy-start.21 = (f32[5,5]{1,0:T(8,128)S(1)}, f32[5,5]{1,0:T(8,128)}, u32[]{:S(2)}) copy-start(f32[5,5]{1,0:T(8,128)} %param.26) | copy-start | bytes 304
  0.0 8.4 %copy-start.23 = (f32[5]{0:T(128)S(1)}, f32[5]{0:T(128)}, u32[]{:S(2)}) copy-start(f32[5]{0:T(128)} %param.27) | copy-start | bytes 64
  7.5 6.4 %collective-permute-start = (f32[6,240,128]{2,1,0:T(8,128)}, f32[6,240,128]{2,1,0:T(8,128)}, u32[]{:S(2)}, u32[]{:S(2)}) collective-permute-start(f32[6,240,128]{2,1,0:T(8,128)} %bitcast.97), channel_id=1, source_target_pairs={{0,1},{1,0},{2,3},{3,2},{4,5},{5,4},{6,7},{7,6},{8,9},{9,8},{10,11... | collective-permute-start | bytes 2211848 | tf_op jit(solution)/shard_map/ppermute | solution.py:514
  9.2 4.7 %copy-start.7 = (f32[288]{0:T(512)S(1)}, f32[288]{0:T(512)}, u32[]{:S(2)}) copy-start(f32[288]{0:T(512)} %constant.86.clone.mix_ref) | copy-start | bytes 3460
  9.2 11.6 %copy-start = (f32[5,32,96,128]{3,2,1,0:T(8,128)S(1)}, f32[5,32,96,128]{3,2,1,0:T(8,128)}, u32[]{:S(2)}) copy-start(f32[5,32,96,128]{3,2,1,0:T(8,128)} %x_ref.2) | copy-start | bytes 23592964
  9.2 11.6 %copy-start.13 = (bf16[96,288]{1,0:T(8,128)(2,1)S(1)}, bf16[96,288]{1,0:T(8,128)(2,1)}, u32[]{:S(2)}) copy-start(bf16[96,288]{1,0:T(8,128)(2,1)} %constant.89.clone.smooth_ref) | copy-start | bytes 165892
  13.9 1.1 %copy-start.1 = (f32[6,5,48,128]{3,2,1,0:T(8,128)S(1)}, f32[6,5,48,128]{3,2,1,0:T(8,128)}, u32[]{:S(2)}) copy-start(f32[6,5,48,128]{3,2,1,0:T(8,128)} %get-tuple-element.44) | copy-start | bytes 2211844
  16.6 17.7 %copy-start.8 = (f32[32,96,128]{2,1,0:T(8,128)S(1)}, f32[32,96,128]{2,1,0:T(8,128)}, u32[]{:S(2)}) copy-start(f32[32,96,128]{2,1,0:T(8,128)} %fwd_ref) | copy-start | bytes 4718596
  16.6 17.7 %copy-start.9 = (f32[32,96,128]{2,1,0:T(8,128)S(1)}, f32[32,96,128]{2,1,0:T(8,128)}, u32[]{:S(2)}) copy-start(f32[32,96,128]{2,1,0:T(8,128)} %bwd_ref) | copy-start | bytes 4718596
  16.6 24.0 %collective-permute-start.1 = (f32[3,240,128]{2,1,0:T(8,128)S(1)}, f32[3,240,128]{2,1,0:T(8,128)S(1)}, u32[]{:S(2)}, u32[]{:S(2)}) collective-permute-start(f32[3,240,128]{2,1,0:T(8,128)S(1)} %get-tuple-element.58), channel_id=1, source_target_pairs={{0,2},{1,3},{2,0},{3,1},{4,6},{5,7},{6,4},{7,5},{8,10},{9,11},{10,... | collective-permute-start | bytes 1105928 | tf_op jit(solution)/shard_map/ppermute | solution.py:528
  19.2 21.3 %collective-permute-start.2 = (f32[3,240,128]{2,1,0:T(8,128)S(1)}, f32[3,240,128]{2,1,0:T(8,128)S(1)}, u32[]{:S(2)}, u32[]{:S(2)}) collective-permute-start(f32[3,240,128]{2,1,0:T(8,128)S(1)} %get-tuple-element.59), channel_id=1, source_target_pairs={{0,4},{1,5},{2,6},{3,7},{4,0},{5,1},{6,2},{7,3},{8,12},{9,13},{10,... | collective-permute-start | bytes 1105928 | tf_op jit(solution)/shard_map/ppermute | solution.py:528
  20.8 19.8 %collective-permute-start.3 = (f32[3,240,128]{2,1,0:T(8,128)S(1)}, f32[3,240,128]{2,1,0:T(8,128)S(1)}, u32[]{:S(2)}, u32[]{:S(2)}) collective-permute-start(f32[3,240,128]{2,1,0:T(8,128)S(1)} %get-tuple-element.60), channel_id=1, source_target_pairs={{0,6},{1,7},{2,4},{3,5},{4,2},{5,3},{6,0},{7,1},{8,14},{9,15},{10,... | collective-permute-start | bytes 1105928 | tf_op jit(solution)/shard_map/ppermute | solution.py:528
  20.8 1.4 %copy-start.10 = (bf16[480,1536]{1,0:T(8,128)(2,1)S(1)}, bf16[480,1536]{1,0:T(8,128)(2,1)}, u32[]{:S(2)}) copy-start(bf16[480,1536]{1,0:T(8,128)(2,1)} %get-tuple-element.53.mixed_ref) | copy-start | bytes 4423684
  22.2 12.1 %copy-start.12 = (bf16[2,384,256]{2,1,0:T(8,128)(2,1)S(1)}, bf16[2,384,256]{2,1,0:T(8,128)(2,1)}, u32[]{:S(2)}) copy-start(bf16[2,384,256]{2,1,0:T(8,128)(2,1)} %constant.103.logs_ref) | copy-start | bytes 1179652
  22.2 12.1 %copy-start.14 = (bf16[256,128]{1,0:T(8,128)(2,1)S(1)}, bf16[256,128]{1,0:T(8,128)(2,1)}, u32[]{:S(2)}) copy-start(bf16[256,128]{1,0:T(8,128)(2,1)} %constant.106.sums_ref) | copy-start | bytes 196612
  22.2 12.1 %copy-start.15 = (bf16[3,16,384]{2,1,0:T(8,128)(2,1)S(1)}, bf16[3,16,384]{2,1,0:T(8,128)(2,1)}, u32[]{:S(2)}) copy-start(bf16[3,16,384]{2,1,0:T(8,128)(2,1)} %constant.98.clone.ends_ref) | copy-start | bytes 110596
  34.3 6.3 %copy-start.2 = (f32[6,5,48,128]{3,2,1,0:T(8,128)S(1)}, f32[6,5,48,128]{3,2,1,0:T(8,128)}, u32[]{:S(2)}) copy-start(f32[6,5,48,128]{3,2,1,0:T(8,128)} %get-tuple-element.44) | copy-start | bytes 2211844
  34.3 6.3 %copy-start.5 = (f32[432]{0:T(512)S(1)}, f32[432]{0:T(512)}, u32[]{:S(2)}) copy-start(f32[432]{0:T(512)} %constant.87.clone.from_ref) | copy-start | bytes 5188
  34.3 6.3 %copy-start.6 = (f32[288]{0:T(512)S(1)}, f32[288]{0:T(512)}, u32[]{:S(2)}) copy-start(f32[288]{0:T(512)} %constant.88.clone.to_ref) | copy-start | bytes 3460
  43.5 2.2 %collective-permute-start.4 = (f32[6,240,128]{2,1,0:T(8,128)S(1)}, f32[6,240,128]{2,1,0:T(8,128)S(1)}, u32[]{:S(2)}, u32[]{:S(2)}) collective-permute-start(f32[6,240,128]{2,1,0:T(8,128)S(1)} %get-tuple-element.64), channel_id=1, source_target_pairs={{0,1},{1,0},{2,3},{3,2},{4,5},{5,4},{6,7},{7,6},{8,9},{9,8},{10,11... | collective-permute-start | bytes 2211848 | tf_op jit(solution)/shard_map/ppermute | solution.py:576
  45.7 4.8 %copy-start.24 = (f32[6,240,128]{2,1,0:T(8,128)}, f32[6,240,128]{2,1,0:T(8,128)S(1)}, u32[]{:S(2)}) copy-start(f32[6,240,128]{2,1,0:T(8,128)S(1)} %collective-permute-done.4) | copy-start | bytes 2211844
  45.7 28.1 %collective-permute-start.7 = (f32[3,32,128]{2,1,0:T(8,128)S(1)}, f32[3,32,128]{2,1,0:T(8,128)S(1)}, u32[]{:S(2)}, u32[]{:S(2)}) collective-permute-start(f32[3,32,128]{2,1,0:T(8,128)S(1)} %get-tuple-element.109), channel_id=1, source_target_pairs={{0,24},{8,16},{16,8},{24,0},{1,25},{9,17},{17,9},{25,1},{2,26},{10... | collective-permute-start | bytes 147464 | tf_op jit(solution)/shard_map/ppermute | solution.py:581
  49.9 24.0 %collective-permute-start.6 = (f32[3,32,128]{2,1,0:T(8,128)S(1)}, f32[3,32,128]{2,1,0:T(8,128)S(1)}, u32[]{:S(2)}, u32[]{:S(2)}) collective-permute-start(f32[3,32,128]{2,1,0:T(8,128)S(1)} %get-tuple-element.109), channel_id=1, source_target_pairs={{0,16},{8,24},{16,0},{24,8},{1,17},{9,25},{17,1},{25,9},{2,18},{10... | collective-permute-start | bytes 147464 | tf_op jit(solution)/shard_map/ppermute | solution.py:581
  49.9 24.0 %collective-permute-start.5 = (f32[3,32,128]{2,1,0:T(8,128)S(1)}, f32[3,32,128]{2,1,0:T(8,128)S(1)}, u32[]{:S(2)}, u32[]{:S(2)}) collective-permute-start(f32[3,32,128]{2,1,0:T(8,128)S(1)} %get-tuple-element.109), channel_id=1, source_target_pairs={{0,8},{8,0},{16,24},{24,16},{1,9},{9,1},{17,25},{25,17},{2,10},{10... | collective-permute-start | bytes 147464 | tf_op jit(solution)/shard_map/ppermute | solution.py:581
  50.5 23.5 %copy-start.20 = (f32[1,3,32,128]{3,2,1,0:T(8,128)S(1)}, f32[1,3,32,128]{3,2,1,0:T(8,128)}, u32[]{:S(2)}) copy-start(f32[1,3,32,128]{3,2,1,0:T(8,128)} %constant.84.clone.1) | copy-start | bytes 147460
  73.9 11.1 %copy-start.19 = (f32[5,32,96]{2,1,0:T(8,128)S(1)}, f32[5,32,96]{2,1,0:T(8,128)}, u32[]{:S(2)}) copy-start(f32[5,32,96]{2,1,0:T(8,128)} %param.22) | copy-start | bytes 184324
  74.0 11.0 %copy-start.3 = (f32[32,96,128]{2,1,0:T(8,128)S(1)}, f32[32,96,128]{2,1,0:T(8,128)}, u32[]{:S(2)}) copy-start(f32[32,96,128]{2,1,0:T(8,128)} %get-tuple-element.51.carry_ref) | copy-start | bytes 4718596
  74.0 11.0 %copy-start.4 = (f32[32,96,128]{2,1,0:T(8,128)S(1)}, f32[32,96,128]{2,1,0:T(8,128)}, u32[]{:S(2)}) copy-start(f32[32,96,128]{2,1,0:T(8,128)} %get-tuple-element.52.tail_ref) | copy-start | bytes 4718596
  74.8 7.1 %collective-permute-start.10 = (f32[5,32,128]{2,1,0:T(8,128)S(1)}, f32[5,32,128]{2,1,0:T(8,128)S(1)}, u32[]{:S(2)}, u32[]{:S(2)}) collective-permute-start(f32[5,32,128]{2,1,0:T(8,128)S(1)} %get-tuple-element.95), channel_id=1, source_target_pairs={{0,24},{8,16},{16,8},{24,0},{1,25},{9,17},{17,9},{25,1},{2,26},{10... | collective-permute-start | bytes 245768 | tf_op jit(solution)/shard_map/ppermute | solution.py:645
  78.6 6.4 %collective-permute-start.9 = (f32[5,32,128]{2,1,0:T(8,128)S(1)}, f32[5,32,128]{2,1,0:T(8,128)S(1)}, u32[]{:S(2)}, u32[]{:S(2)}) collective-permute-start(f32[5,32,128]{2,1,0:T(8,128)S(1)} %get-tuple-element.96), channel_id=1, source_target_pairs={{0,16},{8,24},{16,0},{24,8},{1,17},{9,25},{17,1},{25,9},{2,18},{10... | collective-permute-start | bytes 245768 | tf_op jit(solution)/shard_map/ppermute | solution.py:645
  78.6 6.4 %collective-permute-start.8 = (f32[5,32,128]{2,1,0:T(8,128)S(1)}, f32[5,32,128]{2,1,0:T(8,128)S(1)}, u32[]{:S(2)}, u32[]{:S(2)}) collective-permute-start(f32[5,32,128]{2,1,0:T(8,128)S(1)} %get-tuple-element.94), channel_id=1, source_target_pairs={{0,8},{8,0},{16,24},{24,16},{1,9},{9,1},{17,25},{25,17},{2,10},{10... | collective-permute-start | bytes 245768 | tf_op jit(solution)/shard_map/ppermute | solution.py:645
  (4 other events, 3.3 us)

commit v4 on v3

--- a/solution.py
+++ b/solution.py
@@ -123,11 +123,7 @@
             owner[at] = field
             parts[:, 0, :, at] = states[:, 0, k]
     pick = (owner[None] == np.arange(fields)[:, None]).astype(np.float64)
-    tall = np.concatenate([parts] * fields, axis=2)
-    same = np.repeat(pick, rows, axis=0)
-    tall[:, 2] *= same
-    tall[:, 0] *= same
-    return tall[:, [1, 2, 0]], pick, us, ws
+    return parts[:, [1, 2, 0]], pick, us, ws
 
 
 def split(value):
@@ -161,24 +157,20 @@
     return dot(jnp.concatenate([high, low], axis=1), twice)
 
 
-def mats_kernel(dev_ref, flux_wall_ref, flux_span_ref, visc_ref, wall_rows_ref, wall_cols_ref,
-                wall_ref, span_rows_ref, span_cols_ref, span_ref, wall_out, span_out):
+def mats_kernel(dev_ref, flux_wall_ref, flux_span_ref, visc_ref, wall_cols_ref, wall_ref,
+                span_cols_ref, span_ref, wall_out, span_out):
     exact = functools.partial(jnp.dot, precision=lax.Precision.HIGHEST, preferred_element_type=F32)
-    for flux_ref, rows_ref, cols_ref, ops, out in (
-        (flux_wall_ref, wall_rows_ref, wall_cols_ref, wall_ref[0], wall_out),
-        (flux_span_ref, span_rows_ref, span_cols_ref, span_ref[...], span_out),
+    for flux_ref, cols_ref, ops, out in (
+        (flux_wall_ref, wall_cols_ref, wall_ref[0], wall_out),
+        (flux_span_ref, span_cols_ref, span_ref[...], span_out),
     ):
         cols = cols_ref[...]
-        by_field = exact(-STEP * flux_ref[...], cols)
-        parts = []
-        for _ in range(3):
-            part = by_field.astype(BF16)
-            by_field = by_field - part.astype(F32)
-            parts.append(part.astype(F32))
-        mixing = dot(rows_ref[...], jnp.concatenate(parts, axis=0).astype(BF16))
-        visc = exact(STEP * visc_ref[...], cols)[0:1]
-        high, low = parted(mixing * ops[0] + visc * ops[1] + ops[2])
-        width = cols.shape[1]
+        mixing = exact(-STEP * flux_ref[...], cols)
+        own = exact(STEP * visc_ref[...], cols)[0:1] * ops[1] + ops[2]
+        points, width = own.shape
+        high, low = parted(jnp.concatenate([
+            mixing[field : field + 1] * ops[0] + cols[field : field + 1] * own
+            for field in range(out.shape[0] // points)], axis=0))
         out[:, :width] = high
         out[:, width : 2 * width] = high
         out[:, 2 * width :] = low
@@ -444,9 +436,6 @@
     pad = lambda mat: np.pad(mat, [(0, 0)] * (mat.ndim - 1) + [(0, span_width - n_fields * span)])
     size = 8
     up_to = lambda mat: np.pad(mat, ((0, size - n_fields), (0, 0)))
-    pick_rows = lambda count: jnp.asarray(np.tile(
-        np.pad(np.repeat(np.eye(n_fields), count, axis=0), ((0, 0), (0, size - n_fields))), (1, 3)
-    ).astype(BF16))
     span_cols = pad(np.repeat(np.eye(n_fields), span, axis=1))
     tiny = jnp.zeros((3 * size, size), F32)
     tiny = lax.dynamic_update_slice(tiny, flux_wall, (0, 0))
@@ -466,9 +455,8 @@
                 pl.BlockSpec((size, size), lambda i, dev: (0, 0)),
                 pl.BlockSpec((size, size), lambda i, dev: (1, 0)),
                 pl.BlockSpec((size, size), lambda i, dev: (2, 0)),
-                full_block(lines, 3 * size), full_block(size, width), dev_block(3, lines, width),
-                full_block(all_span, 3 * size), full_block(size, span_width),
-                full_block(3, all_span, span_width)],
+                full_block(size, width), dev_block(3, rows, width), full_block(size, span_width),
+                full_block(3, span, span_width)],
             out_specs=[full_block(lines, 3 * width), full_block(all_span, 3 * span_width)],
         ),
         out_shape=[
@@ -477,12 +465,9 @@
         compiler_params=params(LIMITS["mats"]),
         cost_estimate=cost(10**7, 8 * 10**6),
         name="mats",
-    )(me.astype(jnp.int32).reshape(1), tiny, tiny, tiny, pick_rows(rows), f32(up_to(wall_pick)),
-      f32(wall_ops), pick_rows(span), f32(up_to(span_cols)),
-      f32(np.stack([
-          pad(np.tile(span_ops[1], (n_fields, n_fields))),
-          pad(np.kron(np.eye(n_fields), span_ops[2])),
-          pad(np.kron(np.eye(n_fields), span_ops[0]))])))
+    )(me.astype(jnp.int32).reshape(1), tiny, tiny, tiny, f32(up_to(wall_pick)),
+      f32(wall_ops), f32(up_to(span_cols)),
+      f32(np.stack([pad(np.tile(span_ops[k], (1, n_fields))) for k in (1, 2, 0)])))
     tri = np.triu(np.ones((cells, cells), np.float32))
     ones = np.ones_like(tri)
     twice = lambda mat: np.concatenate([mat, mat], 0)

time: 92.6 us -> 91.9 us (level)
  Pallas kernels: 64.6 us -> 61.8 us
  local copies, waits for them, and re-layouts: 5.21 us -> 7.32 us
    unnamed x50 -> x48, local copies, waits for them, and re-layouts: 4.55 us -> 6.66 us
    pallas_call x1, Pallas kernels: 4.71 us -> 2.96 us  [shards(): pl.pallas_call(mats_kernel, grid_spec=pltpu.PrefetchScalarGridSpec(num_sc...]
  transfers between devices with their start and end apart: 11 -> 11, of which waited for: 3 -> 3; matrix products, arithmetic and copies ran while one was open for 1% -> 1% of each run, Pallas kernels for 50% -> 49%
where the time goes in v4:
time: 91.9 us; the launch traced here: 91.6 us
  Pallas kernels  61.8 us (67%)
  starting transfers between devices  13.9 us (15%)
  waiting for transfers between devices  7.91 us (9%)
  local copies, waits for them, and re-layouts  7.32 us (8%)
    pallas_call x1, Pallas kernels, shards(): pl.pallas_call(functools.partial(sweep_kernel, rows), grid=(span // tile,...  23.3 us
    pallas_call x1, Pallas kernels, shards(): pl.pallas_call(span_kernel, grid=(rows // n_span,), in_specs=[whole(), wh...  12.1 us
    pallas_call x1, Pallas kernels, shards(): pl.pallas_call(taps_kernel, grid=(n_fields,), in_specs=[SMEM, pl.BlockSpe...  7.52 us
    pallas_call x1, Pallas kernels, shards(): pl.pallas_call(close_kernel, grid=(rows // n_close,), in_specs=[gain_bloc...  7.23 us
    unnamed x48, local copies, waits for them, and re-layouts  6.66 us
    pallas_call x1, Pallas kernels, shards(): pl.pallas_call(rates_kernel, grid=(rows // n_rate,), in_specs=[SMEM, whol...  6.22 us
    ppermute x3, waiting for transfers between devices, shards(): lax.ppermute(payload, 'gx', [(at, at ^ hop) for at in range(sections)])  5.68 us
    ppermute x3, starting transfers between devices, shards(): lax.ppermute(gains, 'gx', [(at, at ^ hop) for at in range(sections)])  4.76 us
  transfers between devices with their start and end apart: 11, of which 3 were waited for; matrix products, arithmetic and copies ran while one was open for 1% of the time, Pallas kernels for 49%

profile of v4, /device:TPU:0, one launch (start us, length us, event | category | flops | bytes accessed | tf_op | source)
XLA Modules:
  0.0 91.6 jit_solution(4431050965320496449)
XLA Ops:
  0.0 7.5 %taps.1 = (f32[6,5,48,128]{3,2,1,0:T(8,128)}, f32[6,5,48,128]{3,2,1,0:T(8,128)}) custom-call(f32[1536]{0:T(1024)} %constant.81.clone.taps_ref, f32[5,32,96,128]{3,2,1,0:T(8,128)} %x_ref.2), custom_call_target="tpu_custom_call" | custom-call | flops 23592960 | bytes 7864320 | tf_op jit(solution)/shard_map/taps/pallas_call | solution.py:486
  7.5 0.4 collective-permute-start
  8.0 0.4 dynamic_update_slice.10
  8.4 0.2 dynamic_update_slice.11.flux_wall_ref.flux_span_ref.visc_ref
  8.6 0.6 copy-done.16
  9.2 3.0 %mats.1 = (bf16[160,1152]{1,0:T(8,128)(2,1)}, bf16[480,1536]{1,0:T(8,128)(2,1)}) custom-call(s32[1]{0:T(128)} %bitcast.1.dev_ref, f32[24,8]{1,0:T(8,128)} %copy-done.16, f32[24,8]{1,0:T(8,128)} %copy-done.16, f32[24,8]{1,0:T(8,128)} %copy-done.16, f32[8,384]{1,0:T(8,128)} %constant.86.clone.wall_cols_ref, f32[8,3,32,384]{3,2,1,0:T(8,128)} %constant.87.clone.wall_ref, ...), custom_call_target="tpu_custom_call" | custom-call | flops 10000000 | bytes 8000000 | tf_op jit(solution)/shard_map/mats/pallas_call | solution.py:449
  12.2 1.0 %chip.1 = (f32[3,240,128]{2,1,0:T(8,128)S(1)}, f32[3,240,128]{2,1,0:T(8,128)S(1)}, f32[3,240,128]{2,1,0:T(8,128)S(1)}) custom-call(f32[288]{0:T(512)S(1)} %copy-done.6, f32[6,240,128]{2,1,0:T(8,128)S(1)} %bitcast.83, f32[6,240,128]{2,1,0:T(8,128)S(1)} %collective-permute-done.other_ref), custom_call_target="tpu_custom_call" | custom-call | flops 1105920 | bytes 2211840 | tf_op jit(solution)/shard_map/chip/pallas_call | solution.py:501
  13.2 2.7 %collective-permute-start.1 = (f32[3,240,128]{2,1,0:T(8,128)S(1)}, f32[3,240,128]{2,1,0:T(8,128)S(1)}, u32[]{:S(2)}, u32[]{:S(2)}) collective-permute-start(f32[3,240,128]{2,1,0:T(8,128)S(1)} %get-tuple-element.58), channel_id=1, source_target_pairs={{0,2},{1,3},{2,0},{3,1},{4,6},{5,7},{6,4},{7,5},{8,10},{9,11},{10,... | collective-permute-start | bytes 1105928 | tf_op jit(solution)/shard_map/ppermute | solution.py:513
  15.9 1.5 %collective-permute-start.2 = (f32[3,240,128]{2,1,0:T(8,128)S(1)}, f32[3,240,128]{2,1,0:T(8,128)S(1)}, u32[]{:S(2)}, u32[]{:S(2)}) collective-permute-start(f32[3,240,128]{2,1,0:T(8,128)S(1)} %get-tuple-element.59), channel_id=1, source_target_pairs={{0,4},{1,5},{2,6},{3,7},{4,0},{5,1},{6,2},{7,3},{8,12},{9,13},{10,... | collective-permute-start | bytes 1105928 | tf_op jit(solution)/shard_map/ppermute | solution.py:513
  17.4 0.0 collective-permute-start.3
  17.4 3.2 %copy-done = f32[5,32,96,128]{3,2,1,0:T(8,128)S(1)} copy-done((f32[5,32,96,128]{3,2,1,0:T(8,128)S(1)}, f32[5,32,96,128]{3,2,1,0:T(8,128)}, u32[]{:S(2)}) %copy-start) | copy-done | bytes 7864344
  20.7 1.4 %copy-done.9 = bf16[480,1536]{1,0:T(8,128)(2,1)S(1)} copy-done((bf16[480,1536]{1,0:T(8,128)(2,1)S(1)}, bf16[480,1536]{1,0:T(8,128)(2,1)}, u32[]{:S(2)}) %copy-start.9) | copy-done | bytes 1474584
  22.0 0.0 copy-start.14
  22.1 12.1 %span.1 = (f32[5,32,96,128]{3,2,1,0:T(8,128)}, f32[5,32,96,128]{3,2,1,0:T(8,128)}) custom-call(bf16[96,288]{1,0:T(8,128)(2,1)S(1)} %copy-done.12, bf16[480,1536]{1,0:T(8,128)(2,1)S(1)} %copy-done.9, f32[5,32,96,128]{3,2,1,0:T(8,128)S(1)} %copy-done), custom_call_target="tpu_custom_call" | custom-call | flops 15728640000 | bytes 23592960 | tf_op jit(solution)/shard_map/span/pallas_call | solution.py:519
  34.2 0.0 copy-start.4
  34.2 0.0 copy-start.5
  34.2 6.2 %rates.1 = (f32[32,96,128]{2,1,0:T(8,128)}, f32[32,96,128]{2,1,0:T(8,128)}, f32[32,96,128]{2,1,0:T(8,128)}, f32[32,96,128]{2,1,0:T(8,128)}, f32[32,96,128]{2,1,0...) custom-call(s32[1]{0:T(128)} %bitcast.last_ref, bf16[2,384,256]{2,1,0:T(8,128)(2,1)S(1)} %copy-done.11, ...), custom_call_target="tpu_custom_call" | custom-call | flops 3145728000 | bytes 12582912 | tf_op jit(solution)/shard_map/rates/pallas_call | solution.py:540
  40.5 1.5 %states.1 = (f32[6,240,128]{2,1,0:T(8,128)S(1)}, f32[6,240,128]{2,1,0:T(8,128)S(1)}) custom-call(f32[432]{0:T(512)S(1)} %copy-done.4, f32[288]{0:T(512)S(1)} %copy-done.5, f32[6,240,128]{2,1,0:T(8,128)S(1)} %bitcast.84, f32[6,240,128]{2,1,0:T(8,128)S(1)} %collective-permute-done.other_ref, f32[3,240,128]{2,1,0:T(8,128)S(1)} %collective-permute-done.1.refs_0_, ...), custom_call_target="tpu_custom_call" | custom-call | flops 3686400 | bytes 3686400 | tf_op jit(solution)/shard_map/states/pallas_call | solution.py:552
  42.0 0.9 copy-done.10
  42.9 2.2 %collective-permute-done.4 = f32[6,240,128]{2,1,0:T(8,128)S(1)} collective-permute-done((f32[6,240,128]{2,1,0:T(8,128)S(1)}, f32[6,240,128]{2,1,0:T(8,128)S(1)}, u32[]{:S(2)}, u32[]{:S(2)}) %collective-permute-start.4) | collective-permute-done | bytes 737312 | tf_op jit(solution)/shard_map/ppermute | solution.py:561
  45.1 4.1 %collective-permute-start.7 = (f32[3,32,128]{2,1,0:T(8,128)S(1)}, f32[3,32,128]{2,1,0:T(8,128)S(1)}, u32[]{:S(2)}, u32[]{:S(2)}) collective-permute-start(f32[3,32,128]{2,1,0:T(8,128)S(1)} %get-tuple-element.109), channel_id=1, source_target_pairs={{0,24},{8,16},{16,8},{24,0},{1,25},{9,17},{17,9},{25,1},{2,26},{10... | collective-permute-start | bytes 147464 | tf_op jit(solution)/shard_map/ppermute | solution.py:566
  49.2 0.6 collective-permute-start.5
  49.9 23.3 %sweep.1 = (f32[160,96,128]{2,1,0:T(8,128)S(1)}, f32[160,128]{1,0:T(8,128)}, f32[160,128]{1,0:T(8,128)}) custom-call(bf16[96,288]{1,0:T(8,128)(2,1)} %constant.85.clone.smooth_ref, bf16[480,1536]{1,0:T(8,128)(2,1)} %get-tuple-element.53.mixed_ref, bf16[160,1152]{1,0:T(8,128)(2,1)} %get-tuple-element.67.wall_ref, bf16[2,256,256]{2,1,0:T(8,128)(2,1)} %constant.98.sums_ref, ...), custom_call_target="tpu_custom_call" | custom-call | flops 11796480000 | bytes 23592960 | tf_op jit(solution)/shard_map/sweep/pallas_call | solution.py:610
  73.4 0.1 fusion.11
  73.6 0.5 copy-done.15
  74.0 0.0 copy-done.17
  74.1 3.8 %collective-permute-start.10 = (f32[5,32,128]{2,1,0:T(8,128)S(1)}, f32[5,32,128]{2,1,0:T(8,128)S(1)}, u32[]{:S(2)}, u32[]{:S(2)}) collective-permute-start(f32[5,32,128]{2,1,0:T(8,128)S(1)} %get-tuple-element.95), channel_id=1, source_target_pairs={{0,24},{8,16},{16,8},{24,0},{1,25},{9,17},{17,9},{25,1},{2,26},{10... | collective-permute-start | bytes 245768 | tf_op jit(solution)/shard_map/ppermute | solution.py:630
  77.9 0.6 collective-permute-start.8
  78.6 2.6 %collective-permute-done.10 = f32[5,32,128]{2,1,0:T(8,128)S(1)} collective-permute-done((f32[5,32,128]{2,1,0:T(8,128)S(1)}, f32[5,32,128]{2,1,0:T(8,128)S(1)}, u32[]{:S(2)}, u32[]{:S(2)}) %collective-permute-start.10) | collective-permute-done | bytes 81952 | tf_op jit(solution)/shard_map/ppermute | solution.py:630
  81.2 3.1 %collective-permute-done.9 = f32[5,32,128]{2,1,0:T(8,128)S(1)} collective-permute-done((f32[5,32,128]{2,1,0:T(8,128)S(1)}, f32[5,32,128]{2,1,0:T(8,128)S(1)}, u32[]{:S(2)}, u32[]{:S(2)}) %collective-permute-start.9) | collective-permute-done | bytes 81952 | tf_op jit(solution)/shard_map/ppermute | solution.py:630
  84.3 0.1 multiply_add_fusion
  84.4 7.2 %close.1 = f32[5,32,96,128]{3,2,1,0:T(8,128)} custom-call(f32[32,96,128]{2,1,0:T(8,128)S(1)} %copy-done.2, f32[32,96,128]{2,1,0:T(8,128)S(1)} %copy-done.3, f32[5,32,128]{2,1,0:T(8,128)S(1)} %get-tuple-element.80.enter_ref, f32[5,32,128]{2,1,0:T(8,128)S(1)} %get-tuple-element.79.back_ref, f32[5,32,96,128]{3,2,1,0:T(8,128)S(1)} %bitcast.82), custom_call_target="tpu_custom_call" | custom-call | flops 7864320 | bytes 19660800 | tf_op jit(solution)/shard_map/close/pallas_call | solution.py:639
  (66 shorter events, 0.3 us)
Async XLA Ops:
  0.0 8.0 %copy-start.21 = (f32[5,5]{1,0:T(8,128)S(1)}, f32[5,5]{1,0:T(8,128)}, u32[]{:S(2)}) copy-start(f32[5,5]{1,0:T(8,128)} %param.23) | copy-start | bytes 304
  0.0 8.0 %copy-start.20 = (f32[5,5]{1,0:T(8,128)S(1)}, f32[5,5]{1,0:T(8,128)}, u32[]{:S(2)}) copy-start(f32[5,5]{1,0:T(8,128)} %param.24) | copy-start | bytes 304
  0.0 8.4 %copy-start.22 = (f32[5]{0:T(128)S(1)}, f32[5]{0:T(128)}, u32[]{:S(2)}) copy-start(f32[5]{0:T(128)} %param.25) | copy-start | bytes 64
  7.5 4.7 %copy-start.1 = (f32[6,5,48,128]{3,2,1,0:T(8,128)S(1)}, f32[6,5,48,128]{3,2,1,0:T(8,128)}, u32[]{:S(2)}) copy-start(f32[6,5,48,128]{3,2,1,0:T(8,128)} %get-tuple-element.44) | copy-start | bytes 2211844
  7.5 4.7 %copy-start.6 = (f32[288]{0:T(512)S(1)}, f32[288]{0:T(512)}, u32[]{:S(2)}) copy-start(f32[288]{0:T(512)} %constant.82.clone.mix_ref) | copy-start | bytes 3460
  7.5 4.7 %collective-permute-start = (f32[6,240,128]{2,1,0:T(8,128)}, f32[6,240,128]{2,1,0:T(8,128)S(1)}, u32[]{:S(2)}, u32[]{:S(2)}) collective-permute-start(f32[6,240,128]{2,1,0:T(8,128)} %bitcast.97), channel_id=1, source_target_pairs={{0,1},{1,0},{2,3},{3,2},{4,5},{5,4},{6,7},{7,6},{8,9},{9,8},{10,11... | collective-permute-start | bytes 2211848 | tf_op jit(solution)/shard_map/ppermute | solution.py:499
  9.2 8.2 %copy-start.12 = (bf16[96,288]{1,0:T(8,128)(2,1)S(1)}, bf16[96,288]{1,0:T(8,128)(2,1)}, u32[]{:S(2)}) copy-start(bf16[96,288]{1,0:T(8,128)(2,1)} %constant.85.clone.smooth_ref) | copy-start | bytes 165892
  13.2 27.3 %collective-permute-start.1 = (f32[3,240,128]{2,1,0:T(8,128)S(1)}, f32[3,240,128]{2,1,0:T(8,128)S(1)}, u32[]{:S(2)}, u32[]{:S(2)}) collective-permute-start(f32[3,240,128]{2,1,0:T(8,128)S(1)} %get-tuple-element.58), channel_id=1, source_target_pairs={{0,2},{1,3},{2,0},{3,1},{4,6},{5,7},{6,4},{7,5},{8,10},{9,11},{10,... | collective-permute-start | bytes 1105928 | tf_op jit(solution)/shard_map/ppermute | solution.py:513
  15.9 24.6 %collective-permute-start.2 = (f32[3,240,128]{2,1,0:T(8,128)S(1)}, f32[3,240,128]{2,1,0:T(8,128)S(1)}, u32[]{:S(2)}, u32[]{:S(2)}) collective-permute-start(f32[3,240,128]{2,1,0:T(8,128)S(1)} %get-tuple-element.59), channel_id=1, source_target_pairs={{0,4},{1,5},{2,6},{3,7},{4,0},{5,1},{6,2},{7,3},{8,12},{9,13},{10,... | collective-permute-start | bytes 1105928 | tf_op jit(solution)/shard_map/ppermute | solution.py:513
  17.4 23.1 %collective-permute-start.3 = (f32[3,240,128]{2,1,0:T(8,128)S(1)}, f32[3,240,128]{2,1,0:T(8,128)S(1)}, u32[]{:S(2)}, u32[]{:S(2)}) collective-permute-start(f32[3,240,128]{2,1,0:T(8,128)S(1)} %get-tuple-element.60), channel_id=1, source_target_pairs={{0,6},{1,7},{2,4},{3,5},{4,2},{5,3},{6,0},{7,1},{8,14},{9,15},{10,... | collective-permute-start | bytes 1105928 | tf_op jit(solution)/shard_map/ppermute | solution.py:513
  17.4 3.2 %copy-start = (f32[5,32,96,128]{3,2,1,0:T(8,128)S(1)}, f32[5,32,96,128]{3,2,1,0:T(8,128)}, u32[]{:S(2)}) copy-start(f32[5,32,96,128]{3,2,1,0:T(8,128)} %x_ref.2) | copy-start | bytes 23592964
  20.7 1.4 %copy-start.9 = (bf16[480,1536]{1,0:T(8,128)(2,1)S(1)}, bf16[480,1536]{1,0:T(8,128)(2,1)}, u32[]{:S(2)}) copy-start(bf16[480,1536]{1,0:T(8,128)(2,1)} %get-tuple-element.53.mixed_ref) | copy-start | bytes 4423684
  22.0 12.2 %copy-start.7 = (f32[32,96,128]{2,1,0:T(8,128)S(1)}, f32[32,96,128]{2,1,0:T(8,128)}, u32[]{:S(2)}) copy-start(f32[32,96,128]{2,1,0:T(8,128)} %fwd_ref) | copy-start | bytes 4718596
  22.0 12.2 %copy-start.8 = (f32[32,96,128]{2,1,0:T(8,128)S(1)}, f32[32,96,128]{2,1,0:T(8,128)}, u32[]{:S(2)}) copy-start(f32[32,96,128]{2,1,0:T(8,128)} %bwd_ref) | copy-start | bytes 4718596
  22.0 12.2 %copy-start.11 = (bf16[2,384,256]{2,1,0:T(8,128)(2,1)S(1)}, bf16[2,384,256]{2,1,0:T(8,128)(2,1)}, u32[]{:S(2)}) copy-start(bf16[2,384,256]{2,1,0:T(8,128)(2,1)} %constant.97.logs_ref) | copy-start | bytes 1179652
  22.0 12.2 %copy-start.13 = (bf16[256,128]{1,0:T(8,128)(2,1)S(1)}, bf16[256,128]{1,0:T(8,128)(2,1)}, u32[]{:S(2)}) copy-start(bf16[256,128]{1,0:T(8,128)(2,1)} %constant.100.sums_ref) | copy-start | bytes 196612
  22.0 12.2 %copy-start.14 = (bf16[3,16,384]{2,1,0:T(8,128)(2,1)S(1)}, bf16[3,16,384]{2,1,0:T(8,128)(2,1)}, u32[]{:S(2)}) copy-start(bf16[3,16,384]{2,1,0:T(8,128)(2,1)} %constant.92.clone.ends_ref) | copy-start | bytes 110596
  34.2 6.3 %copy-start.4 = (f32[432]{0:T(512)S(1)}, f32[432]{0:T(512)}, u32[]{:S(2)}) copy-start(f32[432]{0:T(512)} %constant.83.clone.from_ref) | copy-start | bytes 5188
  34.2 6.3 %copy-start.5 = (f32[288]{0:T(512)S(1)}, f32[288]{0:T(512)}, u32[]{:S(2)}) copy-start(f32[288]{0:T(512)} %constant.84.clone.to_ref) | copy-start | bytes 3460
  42.9 2.2 %collective-permute-start.4 = (f32[6,240,128]{2,1,0:T(8,128)S(1)}, f32[6,240,128]{2,1,0:T(8,128)S(1)}, u32[]{:S(2)}, u32[]{:S(2)}) collective-permute-start(f32[6,240,128]{2,1,0:T(8,128)S(1)} %get-tuple-element.64), channel_id=1, source_target_pairs={{0,1},{1,0},{2,3},{3,2},{4,5},{5,4},{6,7},{7,6},{8,9},{9,8},{10,11... | collective-permute-start | bytes 2211848 | tf_op jit(solution)/shard_map/ppermute | solution.py:561
  45.1 4.8 %copy-start.23 = (f32[6,240,128]{2,1,0:T(8,128)}, f32[6,240,128]{2,1,0:T(8,128)S(1)}, u32[]{:S(2)}) copy-start(f32[6,240,128]{2,1,0:T(8,128)S(1)} %collective-permute-done.4) | copy-start | bytes 2211844
  45.1 28.1 %collective-permute-start.7 = (f32[3,32,128]{2,1,0:T(8,128)S(1)}, f32[3,32,128]{2,1,0:T(8,128)S(1)}, u32[]{:S(2)}, u32[]{:S(2)}) collective-permute-start(f32[3,32,128]{2,1,0:T(8,128)S(1)} %get-tuple-element.109), channel_id=1, source_target_pairs={{0,24},{8,16},{16,8},{24,0},{1,25},{9,17},{17,9},{25,1},{2,26},{10... | collective-permute-start | bytes 147464 | tf_op jit(solution)/shard_map/ppermute | solution.py:566
  49.2 24.0 %collective-permute-start.6 = (f32[3,32,128]{2,1,0:T(8,128)S(1)}, f32[3,32,128]{2,1,0:T(8,128)S(1)}, u32[]{:S(2)}, u32[]{:S(2)}) collective-permute-start(f32[3,32,128]{2,1,0:T(8,128)S(1)} %get-tuple-element.109), channel_id=1, source_target_pairs={{0,16},{8,24},{16,0},{24,8},{1,17},{9,25},{17,1},{25,9},{2,18},{10... | collective-permute-start | bytes 147464 | tf_op jit(solution)/shard_map/ppermute | solution.py:566
  49.2 24.0 %collective-permute-start.5 = (f32[3,32,128]{2,1,0:T(8,128)S(1)}, f32[3,32,128]{2,1,0:T(8,128)S(1)}, u32[]{:S(2)}, u32[]{:S(2)}) collective-permute-start(f32[3,32,128]{2,1,0:T(8,128)S(1)} %get-tuple-element.109), channel_id=1, source_target_pairs={{0,8},{8,0},{16,24},{24,16},{1,9},{9,1},{17,25},{25,17},{2,10},{10... | collective-permute-start | bytes 147464 | tf_op jit(solution)/shard_map/ppermute | solution.py:566
  49.9 23.5 %copy-start.19 = (f32[1,3,32,128]{3,2,1,0:T(8,128)S(1)}, f32[1,3,32,128]{3,2,1,0:T(8,128)}, u32[]{:S(2)}) copy-start(f32[1,3,32,128]{3,2,1,0:T(8,128)} %constant.80.clone.1) | copy-start | bytes 147460
  73.2 0.9 %copy-start.17 = (f32[160,128]{1,0:T(8,128)S(1)}, f32[160,128]{1,0:T(8,128)}, u32[]{:S(2)}) copy-start(f32[160,128]{1,0:T(8,128)} %get-tuple-element.77) | copy-start | bytes 245764
  73.2 11.1 %copy-start.18 = (f32[5,32,96]{2,1,0:T(8,128)S(1)}, f32[5,32,96]{2,1,0:T(8,128)}, u32[]{:S(2)}) copy-start(f32[5,32,96]{2,1,0:T(8,128)} %param.20) | copy-start | bytes 184324
  73.3 11.0 %copy-start.2 = (f32[32,96,128]{2,1,0:T(8,128)S(1)}, f32[32,96,128]{2,1,0:T(8,128)}, u32[]{:S(2)}) copy-start(f32[32,96,128]{2,1,0:T(8,128)} %get-tuple-element.51.carry_ref) | copy-start | bytes 4718596
  73.3 11.0 %copy-start.3 = (f32[32,96,128]{2,1,0:T(8,128)S(1)}, f32[32,96,128]{2,1,0:T(8,128)}, u32[]{:S(2)}) copy-start(f32[32,96,128]{2,1,0:T(8,128)} %get-tuple-element.52.tail_ref) | copy-start | bytes 4718596
  74.1 7.1 %collective-permute-start.10 = (f32[5,32,128]{2,1,0:T(8,128)S(1)}, f32[5,32,128]{2,1,0:T(8,128)S(1)}, u32[]{:S(2)}, u32[]{:S(2)}) collective-permute-start(f32[5,32,128]{2,1,0:T(8,128)S(1)} %get-tuple-element.95), channel_id=1, source_target_pairs={{0,24},{8,16},{16,8},{24,0},{1,25},{9,17},{17,9},{25,1},{2,26},{10... | collective-permute-start | bytes 245768 | tf_op jit(solution)/shard_map/ppermute | solution.py:630
  77.9 6.4 %collective-permute-start.9 = (f32[5,32,128]{2,1,0:T(8,128)S(1)}, f32[5,32,128]{2,1,0:T(8,128)S(1)}, u32[]{:S(2)}, u32[]{:S(2)}) collective-permute-start(f32[5,32,128]{2,1,0:T(8,128)S(1)} %get-tuple-element.96), channel_id=1, source_target_pairs={{0,16},{8,24},{16,0},{24,8},{1,17},{9,25},{17,1},{25,9},{2,18},{10... | collective-permute-start | bytes 245768 | tf_op jit(solution)/shard_map/ppermute | solution.py:630
  77.9 6.4 %collective-permute-start.8 = (f32[5,32,128]{2,1,0:T(8,128)S(1)}, f32[5,32,128]{2,1,0:T(8,128)S(1)}, u32[]{:S(2)}, u32[]{:S(2)}) collective-permute-start(f32[5,32,128]{2,1,0:T(8,128)S(1)} %get-tuple-element.94), channel_id=1, source_target_pairs={{0,8},{8,0},{16,24},{24,16},{1,9},{9,1},{17,25},{25,17},{2,10},{10... | collective-permute-start | bytes 245768 | tf_op jit(solution)/shard_map/ppermute | solution.py:630
  (3 other events, 2.3 us)
